TPU v7x, 32 devices: a whole 2x2x4 slice. The times are simulated.
32 devices in a mesh: tm: 16 (over z, y, x), rows: 2 (over core).
Axes of the slice: x: 2, y: 2, z: 4, core: 2. Of those that a mesh axis runs over, the one named last changes fastest.
Arguments:
- frames: bfloat16 [2, 32768, 512], P('rows', 'tm'), may hold values from -6 to 6
- utt_lengths: int32 [2, 128], P('rows'), may hold values from 1 to 64, 2048 in all within a row
- w_qkv: bfloat16 [512, 1536], replicated, may hold values from -0.25 to 0.25
- w_out: bfloat16 [512, 512], replicated, may hold values from -1.5 to 1.5
- w_up: bfloat16 [512, 2048], replicated, may hold values from -0.25 to 0.25
- w_down: bfloat16 [2048, 512], replicated, may hold values from -0.125 to 0.125
- gain_attn: float32 [512], replicated, may hold values from 0.1 to 1.9
- bias_attn: float32 [512], replicated, may hold values from -2.5 to 2.5
- gain_ffn: float32 [512], replicated, may hold values from 0.1 to 1.9
- bias_ffn: float32 [512], replicated, may hold values from -2.5 to 2.5
- out_grad: bfloat16 [2, 32768, 512], P('rows', 'tm'), may hold values from -6 to 6
Outputs:
- out_frames: bfloat16 [2, 32768, 512], P('rows', 'tm')
- grad_frames: float32 [2, 32768, 512], P('rows', 'tm')
- grad_qkv: float32 [512, 1536], replicated
- grad_out_w: float32 [512, 512], replicated
- grad_up: float32 [512, 2048], replicated
- grad_down: float32 [2048, 512], replicated
- grad_gain_attn: float32 [512], replicated
- grad_bias_attn: float32 [512], replicated
- grad_gain_ffn: float32 [512], replicated
- grad_bias_ffn: float32 [512], replicated
Inputs may be any that keep to these rules, and one draw needn't show every extreme that they name: `utt_lengths`: each row's lengths sum to 2048 and the largest is 64.
All inputs are finite; a program needn't handle non-finite values.
Results may differ from a plain program's by a relative error of at most 0.012.
Values may be sent and summed in bfloat16 or wider, within the bound.
A program may use at most 192 MiB of HBM per device.

v0:
```python
import jax
import jax.numpy as jnp
from jax import lax
from jax.sharding import PartitionSpec as P

HEADS = 8
HEAD_DIM = 64


EPS = 1e-05


def from_behind(value, axis, steps):
    count = lax.axis_size(axis)
    initial, last = (max(0, -steps), min(count, count - steps))
    return lax.ppermute(value, axis, [(source, source + steps) for source in range(initial, last)])


def layer_norm(values, gain_vec, shift_vec):
    row_mean = jnp.mean(values, axis=-1, keepdims=True)
    centred = values - row_mean
    row_var = jnp.mean(centred * centred, axis=-1, keepdims=True)
    return centred * lax.rsqrt(row_var + EPS) * gain_vec + shift_vec


def gelu_exact(values):
    return jax.nn.gelu(values, approximate=False)


def inner_rows(first_op, second_op):
    return lax.dot_general(
        first_op, second_op, (((0,), (0,)), ((), ())), preferred_element_type=jnp.float32
    )


def times_t(first_op, second_op):
    return lax.dot_general(
        first_op, second_op, (((1,), (1,)), ((), ())), preferred_element_type=jnp.float32
    )


def attend_mask(seg_ids, groups):
    id_blocks = seg_ids.reshape(groups + 2, 4)
    query_ids = id_blocks[1 : groups + 1]
    key_ids = jnp.concatenate([id_blocks[:groups], id_blocks[1 : groups + 1], id_blocks[2:]], 1)[
        :, 2:10
    ]
    memory_ids = jnp.concatenate([id_blocks[:groups], id_blocks[1 : groups + 1]], 1)
    query_rows = jnp.repeat(query_ids, 16, axis=1)
    key_rows = jnp.repeat(key_ids, 16, axis=1)[:, :120]
    query_seg = lax.broadcasted_iota(jnp.int32, (64, 120), 0) // 16
    key_pos = lax.broadcasted_iota(jnp.int32, (64, 120), 1)
    near_ok = (key_pos >= 16 * query_seg + 2) & (key_pos < 16 * query_seg + 52)
    slot_seg = lax.broadcasted_iota(jnp.int32, (64, 8), 0) // 16
    slot_pos = lax.broadcasted_iota(jnp.int32, (64, 8), 1)
    recent_ok = (slot_pos >= slot_seg) & (slot_pos <= slot_seg + 3)
    memory_ok = recent_ok[None] & (query_rows[:, :, None] == memory_ids[:, None, :])
    frame_ok = near_ok[None] & (query_rows[:, :, None] == key_rows[:, None, :])
    return jnp.concatenate([memory_ok, frame_ok], 2)


def masked_scores(query_heads, key_heads, allowed):
    scores = jnp.einsum(
        "gqhe,gkhe->ghqk", query_heads, key_heads, preferred_element_type=jnp.float32
    ) * HEAD_DIM ** (-0.5)
    return jnp.where(allowed[:, None], scores, -1e30)


def local(
    frames,
    utt_lengths,
    w_qkv,
    w_out,
    w_up,
    w_down,
    gain_attn,
    bias_attn,
    gain_ffn,
    bias_ffn,
    out_grad,
):
    model_width = frames.shape[2]
    frame_count = frames.shape[1]
    groups = frame_count // 64
    seg_count = frame_count // 16
    pair_width = 2 * model_width
    scale_factor = HEAD_DIM ** (-0.5)
    inputs32 = frames[0].astype(jnp.float32)
    norm_one, pull_one = jax.vjp(layer_norm, inputs32, gain_attn, bias_attn)
    normed_low = norm_one.astype(jnp.bfloat16)
    projected = jnp.dot(normed_low, w_qkv, preferred_element_type=jnp.float32).astype(jnp.bfloat16)
    queries = projected[:, :model_width]
    keyvals = projected[:, model_width:]
    w_keyval = w_qkv[:, model_width:]
    summary = jnp.mean(
        normed_low.astype(jnp.float32).reshape(seg_count, 16, model_width), axis=1
    ).astype(jnp.bfloat16)
    memory_kv = jnp.dot(summary, w_keyval, preferred_element_type=jnp.float32).astype(jnp.bfloat16)
    left_kv, left_memory = from_behind(
        (keyvals[frame_count - 30 :], memory_kv[seg_count - 4 :]), "tm", 1
    )
    right_kv = from_behind(keyvals[:4], "tm", -1)
    padded = jnp.concatenate(
        [
            jnp.zeros((2, pair_width), jnp.bfloat16),
            left_kv,
            keyvals,
            right_kv,
            jnp.zeros((28, pair_width), jnp.bfloat16),
        ],
        0,
    )
    frame_blocks = padded.reshape(groups + 1, 64, pair_width)
    frame_window = jnp.concatenate([frame_blocks[:groups], frame_blocks[1:, :56]], 1)
    memory_blocks = jnp.concatenate([left_memory, memory_kv], 0).reshape(groups + 1, 4, pair_width)
    memory_window = jnp.concatenate([memory_blocks[:groups], memory_blocks[1:]], 1)
    key_window = jnp.concatenate([memory_window, frame_window], 1)
    key_heads = key_window[:, :, :model_width].reshape(groups, 128, HEADS, HEAD_DIM)
    value_heads = key_window[:, :, model_width:].reshape(groups, 128, HEADS, HEAD_DIM)
    query_heads = queries.reshape(groups, 64, HEADS, HEAD_DIM)
    first_seg = lax.axis_index("tm") * seg_count
    seg_numbers = first_seg - 4 + lax.iota(jnp.int32, seg_count + 8)
    lengths_row = utt_lengths[0]
    starts = jnp.cumsum(lengths_row) - lengths_row
    seg_ids = jnp.sum((starts[None, :] <= seg_numbers[:, None]).astype(jnp.int32), axis=1) - 1
    inside = (seg_numbers >= 0) & (seg_numbers < seg_count * lax.axis_size("tm"))
    seg_ids = jnp.where(inside, seg_ids, -1)
    allowed = attend_mask(seg_ids, groups)
    scores = masked_scores(query_heads, key_heads, allowed)
    top_score = jnp.max(scores, axis=-1, keepdims=True)
    shifted = jnp.exp(scores - top_score)
    totals = jnp.sum(shifted, axis=-1, keepdims=True)
    log_total = top_score + jnp.log(totals)
    probs_low = (shifted / totals).astype(jnp.bfloat16)
    attended = jnp.einsum(
        "ghqk,gkhe->gqhe", probs_low, value_heads, preferred_element_type=jnp.float32
    )
    attn_low = attended.reshape(frame_count, model_width).astype(jnp.bfloat16)
    middle = inputs32 + jnp.dot(attn_low, w_out, preferred_element_type=jnp.float32)
    norm_two, pull_two = jax.vjp(layer_norm, middle, gain_ffn, bias_ffn)
    normed_two = norm_two.astype(jnp.bfloat16)
    hidden = jnp.dot(normed_two, w_up, preferred_element_type=jnp.float32)
    activated, pull_act = jax.vjp(gelu_exact, hidden)
    act_low = activated.astype(jnp.bfloat16)
    result = middle + jnp.dot(act_low, w_down, preferred_element_type=jnp.float32)
    grad_low = out_grad[0]
    grad_down = inner_rows(act_low, grad_low)
    (d_hidden,) = pull_act(times_t(grad_low, w_down))
    d_hidden_low = d_hidden.astype(jnp.bfloat16)
    grad_up = inner_rows(normed_two, d_hidden_low)
    d_two = times_t(d_hidden_low, w_up)
    d_mid_norm, grad_gain_ffn, grad_bias_ffn = pull_two(d_two)
    d_middle = grad_low.astype(jnp.float32) + d_mid_norm
    d_branch = d_middle.astype(jnp.bfloat16)
    grad_out_w = inner_rows(attn_low, d_branch)
    d_att = times_t(d_branch, w_out).astype(jnp.bfloat16).reshape(groups, 64, HEADS, HEAD_DIM)
    again = masked_scores(query_heads, key_heads, allowed)
    probs_back = jnp.exp(again - log_total)
    probs_back_low = probs_back.astype(jnp.bfloat16)
    d_probs = jnp.einsum("gqhe,gkhe->ghqk", d_att, value_heads, preferred_element_type=jnp.float32)
    row_dots = jnp.sum(probs_back * d_probs, axis=-1, keepdims=True)
    d_scores = (probs_back * (d_probs - row_dots)).astype(jnp.bfloat16)
    d_query = (
        jnp.einsum("ghqk,gkhe->gqhe", d_scores, key_heads, preferred_element_type=jnp.float32)
        * scale_factor
    )
    d_key = (
        jnp.einsum("ghqk,gqhe->gkhe", d_scores, query_heads, preferred_element_type=jnp.float32)
        * scale_factor
    )
    d_value = jnp.einsum(
        "ghqk,gqhe->gkhe", probs_back_low, d_att, preferred_element_type=jnp.float32
    )
    d_window = jnp.concatenate(
        [d_key.reshape(groups, 128, model_width), d_value.reshape(groups, 128, model_width)], 2
    )
    d_memwin = d_window[:, :8]
    d_framewin = d_window[:, 8:]
    d_frames_pad = (
        jnp.pad(d_framewin[:, :64], ((0, 1), (0, 0), (0, 0)))
        + jnp.pad(d_framewin[:, 64:], ((1, 0), (0, 8), (0, 0)))
    ).reshape(frame_count + 64, pair_width)
    d_memory_pad = (
        jnp.pad(d_memwin[:, :4], ((0, 1), (0, 0), (0, 0)))
        + jnp.pad(d_memwin[:, 4:], ((1, 0), (0, 0), (0, 0)))
    ).reshape(seg_count + 4, pair_width)
    back_left, back_memory = (
        from_behind(d_frames_pad[2:32].astype(jnp.bfloat16), "tm", -1).astype(jnp.float32),
        from_behind(d_memory_pad[:4].astype(jnp.bfloat16), "tm", -1).astype(jnp.float32),
    )
    back_right = from_behind(d_frames_pad[frame_count + 32 : frame_count + 36], "tm", 1)
    d_keyvals = (
        d_frames_pad[32 : frame_count + 32]
        + jnp.pad(back_right, ((0, frame_count - 4), (0, 0)))
        + jnp.pad(back_left, ((frame_count - 30, 0), (0, 0)))
    )
    d_memory = d_memory_pad[4:] + jnp.pad(back_memory, ((seg_count - 4, 0), (0, 0)))
    d_proj_low = jnp.concatenate(
        [
            d_query.reshape(frame_count, model_width).astype(jnp.bfloat16),
            d_keyvals.astype(jnp.bfloat16),
        ],
        1,
    )
    d_memory_low = d_memory.astype(jnp.bfloat16)
    grad_qkv = inner_rows(normed_low, d_proj_low) + jnp.pad(
        inner_rows(summary, d_memory_low), ((0, 0), (model_width, 0))
    )
    d_summary = times_t(d_memory_low, w_keyval) * (1.0 / 16)
    d_normed = (
        times_t(d_proj_low, w_qkv).reshape(seg_count, 16, model_width) + d_summary[:, None, :]
    ).reshape(frame_count, model_width)
    d_input_norm, grad_gain_attn, grad_bias_attn = pull_one(d_normed)
    grad_inputs = d_middle + d_input_norm
    (
        grad_qkv,
        grad_out_w,
        grad_gain_attn,
        grad_bias_attn,
        grad_up,
        grad_down,
        grad_gain_ffn,
        grad_bias_ffn,
    ) = lax.psum(
        (
            grad_qkv,
            grad_out_w,
            grad_gain_attn,
            grad_bias_attn,
            grad_up,
            grad_down,
            grad_gain_ffn,
            grad_bias_ffn,
        ),
        ("tm", "rows"),
    )
    return (
        result.astype(jnp.bfloat16)[None],
        grad_inputs[None],
        grad_qkv,
        grad_out_w,
        grad_up,
        grad_down,
        grad_gain_attn,
        grad_bias_attn,
        grad_gain_ffn,
        grad_bias_ffn,
    )


def solution(mesh):
    in_specs = (
        P("rows", "tm", None),
        P("rows", None),
        P(),
        P(),
        P(),
        P(),
        P(),
        P(),
        P(),
        P(),
        P("rows", "tm", None),
    )
    out_specs = (
        P("rows", "tm", None),
        P("rows", "tm", None),
        P(),
        P(),
        P(),
        P(),
        P(),
        P(),
        P(),
        P(),
    )
    return jax.shard_map(local, mesh=mesh, in_specs=in_specs, out_specs=out_specs, check_vma=False)
```

profile of v0, /device:TPU:0, one launch (start us, length us, event | category | flops | bytes accessed | tf_op | source)
XLA Modules:
  0.0 669.5 jit_solution(7022413303375876797)
XLA Ops:
  48.9 6.3 reshape.292
  55.2 6.8 %copy.132 = bf16[32,64,8,64]{1,3,2,0:T(8,128)(2,1)} copy(bf16[32,64,8,64]{3,2,1,0:T(8,128)(2,1)} %reshape.292) | data formatting | bytes 4194304 | tf_op jit(solution)/shard_map/reshape | solution.py:120
  66.2 21.9 %concatenate.29 = bf16[2112,1024]{1,0:T(8,128)(2,1)} concatenate(bf16[2,1024]{1,0:T(2,128)(2,1)S(1)} %broadcast_in_dim.38, bf16[30,1024]{1,0:T(8,128)(2,1)S(1)} %collective-permute-done.1, bf16[2048,1024]{1,0:T(8,128)(2,1)} %slice.140, bf16[4,1024]{1,0:T(4,128)(2,1)S(1)} %collective-permute-done.2, bf16[28,1024]{1,0:T(8,128)(2,1)S(1)} %broadcast_in_dim.39), dimensions={0} | concatenate | bytes 8650752 | tf_op jit(solution)/shard_map/concatenate | solution.py:103
  92.4 19.9 %concatenate.28 = bf16[2080,1024]{1,0:T(8,128)(2,1)} concatenate(bf16[2,1024]{1,0:T(2,128)(2,1)S(1)} %broadcast_in_dim.38, bf16[30,1024]{1,0:T(8,128)(2,1)S(1)} %collective-permute-done.1, bf16[2048,1024]{1,0:T(8,128)(2,1)} %slice.140), dimensions={0} | concatenate | bytes 8519680 | tf_op jit(solution)/shard_map/concatenate | solution.py:103
  122.2 6.4 copy.124
  128.6 6.4 copy.117
  135.0 7.3 %fusion.54 = (f32[32,8,64]{2,1,0:T(8,128)S(1)}, f32[32,8,64,128]{3,2,1,0:T(8,128)S(1)}) fusion(bf16[32,64,8,64]{1,3,2,0:T(8,128)(2,1)} %copy.132, bf16[32,128,8,64]{1,3,2,0:T(8,128)(2,1)} %bitcast.88, pred[32,64,128]{2,1,0:T(8,128)(4,1)S(1)} %pad_add_fusion.1), kind=kOutput, calls=%fused_computation.142 | convolution fusion | flops 274710528 | bytes 15007744 | tf_op jit(solution)/shard_map/gqhe,gkhe->ghqk/dot_general | solution.py:63
  147.8 7.5 %convert_bitcast_fusion = bf16[32,64,8,64]{1,3,2,0:T(8,128)(2,1)} fusion(bf16[32,128,8,64]{1,3,2,0:T(8,128)(2,1)S(1)} %bitcast.96, f32[32,8,64,128]{3,2,1,0:T(8,128)S(1)} %get-tuple-element.86, f32[32,8,64]{2,1,0:T(8,128)S(1)} %fusion.9, f32[32,8,64]{2,1,0:T(8,128)S(1)} %get-tuple-element.85), kind=kOutput, calls=%fused_computation.57 | convolution fusion | flops 275775488 | bytes 14811136 | tf_op jit(solution)/shard_map/ghqk,gkhe->gqhe/dot_general | solution.py:135
  155.3 6.8 %copy.126 = bf16[32,64,8,64]{3,2,1,0:T(8,128)(2,1)} copy(bf16[32,64,8,64]{1,3,2,0:T(8,128)(2,1)} %convert_bitcast_fusion) | data formatting | bytes 4194304 | tf_op jit(solution)/shard_map/convert_element_type | solution.py:138
  162.1 6.7 convert_element_type.134
  174.1 44.0 %multiply_convert_fusion = (bf16[2048,2048]{1,0:T(8,128)(2,1)}, f32[2048,2048]{1,0:T(8,128)}, f32[2048,2048]{1,0:T(8,128)}) fusion(bf16[512,2048]{1,0:T(8,128)(2,1)S(1)} %copy-done, f32[2048,512]{0,1:T(8,128)S(1)} %get-tuple-element.88, f32[512]{0:T(512)S(1)} %copy-done.55, f32[512]{0:T(512)S(1)} %copy-done.51, f32[2048]{0:T(1024)S(1)} %fusion.39, ...), kind=kOutput, calls=%fused_computation.9 | convolution fusion | flops 4572839936 | bytes 48254976 | tf_op jit(solution)/shard_map/dot_general | solution.py:142
  218.1 20.7 %add_convert_fusion = bf16[2048,2048]{1,0:T(8,128)(2,1)} fusion(f32[2048,2048]{1,0:T(8,128)} %get-tuple-element.77, f32[2048,2048]{1,0:T(8,128)} %get-tuple-element.89, bf16[2048,512]{1,0:T(8,128)(2,1)} %param.16, bf16[1,2048,512]{2,1,0:T(8,128)(2,1)} %param.21), kind=kOutput, calls=%fused_computation.8 | convolution fusion | flops 4353687552 | bytes 46137344 | tf_op jit(solution)/shard_map/dot_general | solution.py:37
  238.9 10.2 %fusion.56 = (f32[512]{0:T(512)}, f32[2048,512]{1,0:T(8,128)}) fusion(bf16[2048,2048]{1,0:T(8,128)(2,1)} %add_convert_fusion, bf16[512,2048]{1,0:T(8,128)(2,1)S(1)} %copy-done), kind=kOutput, calls=%fused_computation.144 | convolution fusion | flops 4296015360 | bytes 14682112 | tf_op jit(solution)/shard_map/dot_general | solution.py:37
  254.5 5.4 multiply_reduce_fusion.1
  270.4 6.8 %copy.133 = bf16[32,64,8,64]{1,3,2,0:T(8,128)(2,1)} copy(bf16[32,64,8,64]{3,2,1,0:T(8,128)(2,1)} %reshape.294) | data formatting | bytes 4194304 | tf_op jit(solution)/shard_map/reshape | solution.py:156
  277.3 10.1 %multiply_reduce_fusion = (f32[32,8,64]{2,1,0:T(8,128)S(1)}, f32[32,8,64,128]{3,2,1,0:T(8,128)}) fusion(f32[32,8,64,128]{3,2,1,0:T(8,128)} %copy-done.4, f32[32,8,64]{2,1,0:T(8,128)S(1)} %copy-done.34, bf16[32,64,8,64]{1,3,2,0:T(8,128)(2,1)} %copy.133, bf16[32,128,8,64]{1,3,2,0:T(8,128)(2,1)} %bitcast.95), kind=kOutput, calls=%fused_computation.31 | convolution fusion | flops 274710528 | bytes 23199744 | tf_op jit(solution)/shard_map/gqhe,gkhe->ghqk/dot_general | solution.py:160
  287.4 7.8 %multiply_convert_fusion.2 = bf16[32,8,64,128]{3,2,1,0:T(8,128)(2,1)S(1)} fusion(f32[32,8,64,128]{3,2,1,0:T(8,128)} %get-tuple-element.91, f32[32,8,64,128]{3,2,1,0:T(8,128)} %copy-done.4, f32[32,8,64]{2,1,0:T(8,128)S(1)} %get-tuple-element.90, f32[32,8,64]{2,1,0:T(8,128)S(1)} %copy-done.34), kind=kLoop, calls=%fused_computation.30 | loop fusion | flops 8388608 | bytes 21102592 | tf_op jit(solution)/shard_map/convert_element_type | solution.py:162
  299.6 5.5 broadcast_multiply_fusion
  310.9 9.0 %copy.134 = f32[32,128,512]{2,1,0:T(8,128)} copy(f32[32,128,512]{1,2,0:T(8,128)} %bitcast.87) | data formatting | bytes 16777216 | tf_op jit(solution)/shard_map/reshape | solution.py:175
  320.0 9.1 %copy.135 = f32[32,128,512]{2,1,0:T(8,128)} copy(f32[32,128,512]{1,2,0:T(8,128)} %bitcast.93) | data formatting | bytes 16777216 | tf_op jit(solution)/shard_map/reshape | solution.py:175
  329.1 7.0 %fusion.6 = f32[32,64,1024]{2,1,0:T(8,128)} fusion(f32[32,128,512]{2,1,0:T(8,128)} %copy.134, f32[32,128,512]{2,1,0:T(8,128)} %copy.135), kind=kLoop, calls=%fused_computation.24 | loop fusion | flops 2097152 | bytes 25165824 | tf_op jit(solution)/shard_map/concatenate | solution.py:174
  345.7 10.1 %fusion.47 = f32[512,2048]{1,0:T(8,128)} fusion(bf16[2048,2048]{1,0:T(8,128)(2,1)} %add_convert_fusion, f32[2048,512]{0,1:T(8,128)S(1)} %copy-done.9, f32[512]{0:T(512)S(1)} %copy-done.55, f32[512]{0:T(512)S(1)} %copy-done.51, f32[2048]{0:T(1024)S(1)} %fusion.39, f32[2048]{0:T(1024)S(1)} %broadcast_multiply_fusion.1), kind=kOutput, calls=%fused_computation.136 | convolution fusion | flops 4300210176 | bytes 16797696 | tf_op jit(solution)/shard_map/dot_general | solution.py:31
  361.1 6.1 fusion.23
  367.2 11.7 %pad_add_fusion = f32[33,64,1024]{2,1,0:T(8,128)} fusion(f32[32,56,1024]{2,1,0:T(8,128)} %fusion.10, f32[32,64,1024]{2,1,0:T(8,128)} %fusion.6), kind=kLoop, calls=%fused_computation.23 | loop fusion | flops 2162688 | bytes 24379392 | tf_op jit(solution)/shard_map/add | solution.py:180
  380.6 6.8 %copy.131 = bf16[32,64,8,64]{3,2,1,0:T(8,128)(2,1)} copy(bf16[32,64,8,64]{1,3,2,0:T(8,128)(2,1)} %fusion.14) | data formatting | bytes 4194304 | tf_op jit(solution)/shard_map/convert_element_type | solution.py:200
  387.3 6.6 convert_element_type.145
  413.3 11.2 %fusion.21 = bf16[1,2048,512]{1,2,0:T(8,128)(2,1)} fusion(f32[2048,512]{0,1:T(8,128)} %copy-done.7, bf16[2048,2048]{1,0:T(8,128)(2,1)} %get-tuple-element.76, bf16[2048,512]{1,0:T(8,128)(2,1)} %param.16), kind=kOutput, calls=%fused_computation.70 | convolution fusion | flops 4297064448 | bytes 16777216 | tf_op jit(solution)/shard_map/dot_general | solution.py:145
  432.8 5.6 copy.137
  438.4 8.5 %fusion.49 = (f32[512]{0:T(512)S(1)}, f32[2048]{0:T(1024)S(1)}, f32[2048,512]{0,1:T(8,128)S(1)}) fusion(f32[512]{0:T(512)S(1)} %copy-done.49, f32[2048]{0:T(1024)S(1)} %copy-done.39, bf16[1,2048,512]{1,2,0:T(8,128)(2,1)S(1)} %copy-done.6, f32[2048,512]{0,1:T(8,128)} %copy.137, bf16[512,1536]{1,0:T(8,128)(2,1)} %param.13, ...), kind=kOutput, calls=%fused_computation.138 | convolution fusion | flops 3241145856 | bytes 18370560 | tf_op jit(solution)/shard_map/dot_general | solution.py:37
  453.8 5.5 copy.140
  459.3 45.5 %all-reduce.8 = (f32[512]{0:T(512)}, f32[512]{0:T(512)}, f32[512]{0:T(512)}, f32[512]{0:T(512)}) all-reduce(f32[512]{0:T(512)S(1)} %get-tuple-element.62, f32[512]{0:T(512)S(1)} %get-tuple-element.64, f32[512]{0:T(512)S(1)} %copy-done.50, f32[512]{0:T(512)S(1)} %copy-done.54), channel_id=1, replica_groups=mesh['tm'=16,'rows'=2] {'tm','rows'}, use_global_device_ids=true, to_apply=%region_19.20 | all-reduce | flops 2048 | bytes 16384 | tf_op jit(solution)/shard_map/psum | solution.py:224
  504.9 146.7 %all-reduce.12.cloned.1.call-done = (f32[512,1536]{1,0:T(8,128)}, f32[512,512]{1,0:T(8,128)}, f32[512,2048]{1,0:T(8,128)}, f32[2048,512]{1,0:T(8,128)}) async-done(((f32[512,1536]{1,0:T(8,128)}, f32[512,512]{1,0:T(8,128)}, f32[512,2048]{1,0:T(8,128)}, f32[2048,512]{1,0:T(8,128)}), (f32[512,1536]{1,0:T(8,128)}, f32[512,512]{1,0:T(8,128)}, f32[512,2048]{1,0:T(8,128)}, ...) | async-done | bytes 12582928 | tf_op jit(solution)/shard_map/psum | solution.py:224
  (228 shorter events, 158.1 us)
Async XLA Ops:
  7.2 166.9 %copy-start = (bf16[512,2048]{1,0:T(8,128)(2,1)S(1)}, bf16[512,2048]{1,0:T(8,128)(2,1)}, u32[]{:S(2)}) copy-start(bf16[512,2048]{1,0:T(8,128)(2,1)} %param.15) | copy-start | bytes 6291460
  7.2 8.4 %copy-start.48 = (f32[512]{0:T(512)S(1)}, f32[512]{0:T(512)}, u32[]{:S(2)}) copy-start(f32[512]{0:T(512)} %param.17) | copy-start | bytes 6148
  7.2 8.4 %copy-start.52 = (f32[512]{0:T(512)S(1)}, f32[512]{0:T(512)}, u32[]{:S(2)}) copy-start(f32[512]{0:T(512)} %param.18) | copy-start | bytes 6148
  7.2 644.3 %all-reduce.12.cloned.1.call-start = ((), (), s32[]{:S(2)}) async-start(), calls=%async_computation | async-start | bytes 25165824 | tf_op jit(solution)/shard_map/psum | solution.py:224
  13.4 12.8 %copy-start.38 = (f32[2048]{0:T(1024)}, f32[2048]{0:T(1024)S(1)}, u32[]{:S(2)}) copy-start(f32[2048]{0:T(1024)S(1)} %broadcast_multiply_fusion.2) | copy-start | bytes 24580
  15.7 10.4 %copy-start.40 = (f32[2048]{0:T(1024)}, f32[2048]{0:T(1024)S(1)}, u32[]{:S(2)}) copy-start(f32[2048]{0:T(1024)S(1)} %fusion.38) | copy-start | bytes 24580
  19.9 46.3 %collective-permute-start.1 = (bf16[30,1024]{1,0:T(8,128)(2,1)S(1)}, bf16[30,1024]{1,0:T(8,128)(2,1)S(1)}, u32[]{:S(2)}, u32[]{:S(2)}) collective-permute-start(bf16[30,1024]{1,0:T(8,128)(2,1)S(1)} %slice.139), channel_id=1, source_target_pairs={{0,2},{2,4},{4,6},{6,8},{8,10},{10,12},{12,14},{14,16},{16,18},{18... | collective-permute-start | bytes 184328 | tf_op jit(solution)/shard_map/ppermute | solution.py:16
  24.8 41.4 %collective-permute-start.2 = (bf16[4,1024]{1,0:T(4,128)(2,1)S(1)}, bf16[4,1024]{1,0:T(4,128)(2,1)S(1)}, u32[]{:S(2)}, u32[]{:S(2)}) collective-permute-start(bf16[4,1024]{1,0:T(4,128)(2,1)S(1)} %slice.142), channel_id=1, source_target_pairs={{2,0},{4,2},{6,4},{8,6},{10,8},{12,10},{14,12},{16,14},{18,16},{20... | collective-permute-start | bytes 24584 | tf_op jit(solution)/shard_map/ppermute | solution.py:16
  30.4 8.5 %copy-start.56 = (s32[1,128]{1,0:T(1,128)S(1)}, s32[1,128]{1,0:T(1,128)}, u32[]{:S(2)}) copy-start(s32[1,128]{1,0:T(1,128)} %param.12) | copy-start | bytes 1540
  34.2 31.8 %collective-permute-start = (bf16[4,1024]{1,0:T(4,128)(2,1)S(1)}, bf16[4,1024]{1,0:T(4,128)(2,1)S(1)}, u32[]{:S(2)}, u32[]{:S(2)}) collective-permute-start(bf16[4,1024]{1,0:T(4,128)(2,1)S(1)} %slice.138), channel_id=1, source_target_pairs={{0,2},{2,4},{4,6},{6,8},{8,10},{10,12},{12,14},{14,16},{16,18},{18... | collective-permute-start | bytes 24584 | tf_op jit(solution)/shard_map/ppermute | solution.py:16
  162.1 6.7 %copy-start.36 = (bf16[512,512]{1,0:T(8,128)(2,1)S(1)}, bf16[512,512]{1,0:T(8,128)(2,1)}, u32[]{:S(2)}) copy-start(bf16[512,512]{1,0:T(8,128)(2,1)} %param.14) | copy-start | bytes 1572868
  172.5 45.7 %copy-start.7 = (f32[2048,512]{0,1:T(8,128)}, f32[2048,512]{0,1:T(8,128)S(1)}, u32[]{:S(2)}) copy-start(f32[2048,512]{0,1:T(8,128)S(1)} %get-tuple-element.88) | copy-start | bytes 12582916
  270.4 6.9 %copy-start.34 = (f32[32,8,64]{2,1,0:T(8,128)S(1)}, f32[32,8,64]{2,1,0:T(8,128)}, u32[]{:S(2)}) copy-start(f32[32,8,64]{2,1,0:T(8,128)} %log_add_fusion) | copy-start | bytes 196612
  287.4 7.8 %copy-start.12 = (bf16[32,128,512]{1,2,0:T(8,128)(2,1)S(1)}, bf16[32,128,512]{1,2,0:T(8,128)(2,1)}, u32[]{:S(2)}) copy-start(bf16[32,128,512]{1,2,0:T(8,128)(2,1)} %copy.124) | copy-start | bytes 12582916
  295.2 9.8 %slice-start = ((s8[8388608]{0:T(1024)(128)(4,1)}), s8[4194304]{0:T(1024)(128)(4,1)S(1)}, s32[]{:S(2)}) async-start(s8[8388608]{0:T(1024)(128)(4,1)} %bitcast.85), calls=%async_computation.1 | async-start | bytes 8388608
  329.1 8.8 %copy-start.2 = (f32[32,128,512]{2,1,0:T(8,128)S(1)}, f32[32,128,512]{2,1,0:T(8,128)}, u32[]{:S(2)}) copy-start(f32[32,128,512]{2,1,0:T(8,128)} %copy.134) | copy-start | bytes 25165828
  329.1 11.1 %copy-start.3 = (f32[32,128,512]{2,1,0:T(8,128)S(1)}, f32[32,128,512]{2,1,0:T(8,128)}, u32[]{:S(2)}) copy-start(f32[32,128,512]{2,1,0:T(8,128)} %copy.135) | copy-start | bytes 25165828
  345.6 10.1 %copy-start.19 = (bf16[2048,512]{1,0:T(8,128)(2,1)S(1)}, bf16[2048,512]{1,0:T(8,128)(2,1)}, u32[]{:S(2)}) copy-start(bf16[2048,512]{1,0:T(8,128)(2,1)} %convert_element_type.134) | copy-start | bytes 6291460
  345.6 10.1 %copy-start.32 = (bf16[2048,512]{0,1:T(8,128)(2,1)S(1)}, bf16[2048,512]{0,1:T(8,128)(2,1)}, u32[]{:S(2)}) copy-start(bf16[2048,512]{0,1:T(8,128)(2,1)} %copy-done.31) | copy-start | bytes 6291460
  358.3 22.3 %copy-start.29 = (f32[33,4,1024]{2,1,0:T(4,128)}, f32[33,4,1024]{2,1,0:T(4,128)S(1)}, u32[]{:S(2)}) copy-start(f32[33,4,1024]{2,1,0:T(4,128)S(1)} %fusion.29) | copy-start | bytes 1622020
  358.3 42.1 %collective-permute-start.5 = (bf16[4,1024]{1,0:T(4,128)(2,1)S(1)}, bf16[4,1024]{1,0:T(4,128)(2,1)S(1)}, u32[]{:S(2)}, u32[]{:S(2)}) collective-permute-start(bf16[4,1024]{1,0:T(4,128)(2,1)S(1)} %fusion.37), channel_id=1, source_target_pairs={{2,0},{4,2},{6,4},{8,6},{10,8},{12,10},{14,12},{16,14},{18,16},{20... | collective-permute-start | bytes 24584 | tf_op jit(solution)/shard_map/ppermute | solution.py:16
  387.3 12.8 %slice-start.3 = ((f32[33,4,1024]{2,1,0:T(4,128)}), f32[32,4,1024]{2,1,0:T(4,128)S(1)}, s32[]{:S(2)}) async-start(f32[33,4,1024]{2,1,0:T(4,128)} %copy-done.29), calls=%async_computation.4 | async-start | bytes 1048576 | tf_op jit(solution)/shard_map/slice | solution.py:197
  387.3 13.0 %copy-start.28 = (f32[128,512]{1,0:T(8,128)S(1)}, f32[128,512]{1,0:T(8,128)}, u32[]{:S(2)}) copy-start(f32[128,512]{1,0:T(8,128)} %copy-done.27) | copy-start | bytes 786436
  393.9 7.7 %collective-permute-start.4 = (bf16[30,1024]{1,0:T(8,128)(2,1)S(1)}, bf16[30,1024]{1,0:T(8,128)(2,1)S(1)}, u32[]{:S(2)}, u32[]{:S(2)}) collective-permute-start(bf16[30,1024]{1,0:T(8,128)(2,1)S(1)} %slice.193), channel_id=1, source_target_pairs={{2,0},{4,2},{6,4},{8,6},{10,8},{12,10},{14,12},{16,14},{18,16},{20... | collective-permute-start | bytes 184328 | tf_op jit(solution)/shard_map/ppermute | solution.py:16
  395.2 6.4 collective-permute-start.3
  400.8 7.2 %copy-start.6 = (bf16[1,2048,512]{1,2,0:T(8,128)(2,1)S(1)}, bf16[1,2048,512]{1,2,0:T(8,128)(2,1)}, u32[]{:S(2)}) copy-start(bf16[1,2048,512]{1,2,0:T(8,128)(2,1)} %copy.115) | copy-start | bytes 6291460
  400.8 7.1 %copy-start.30 = (bf16[2048,512]{1,0:T(8,128)(2,1)S(1)}, bf16[2048,512]{1,0:T(8,128)(2,1)}, u32[]{:S(2)}) copy-start(bf16[2048,512]{1,0:T(8,128)(2,1)} %convert_element_type.145) | copy-start | bytes 6291460
  400.9 7.1 %copy-start.39 = (f32[2048]{0:T(1024)S(1)}, f32[2048]{0:T(1024)}, u32[]{:S(2)}) copy-start(f32[2048]{0:T(1024)} %copy-done.38) | copy-start | bytes 24580
  400.9 7.1 %copy-start.41 = (f32[2048]{0:T(1024)S(1)}, f32[2048]{0:T(1024)}, u32[]{:S(2)}) copy-start(f32[2048]{0:T(1024)} %copy-done.40) | copy-start | bytes 24580
  400.9 7.1 %copy-start.49 = (f32[512]{0:T(512)S(1)}, f32[512]{0:T(512)}, u32[]{:S(2)}) copy-start(f32[512]{0:T(512)} %param.17) | copy-start | bytes 6148
  400.9 7.1 %copy-start.53 = (f32[512]{0:T(512)S(1)}, f32[512]{0:T(512)}, u32[]{:S(2)}) copy-start(f32[512]{0:T(512)} %param.18) | copy-start | bytes 6148
  438.4 8.5 %copy-start.45 = (f32[2048]{0:T(1024)S(1)}, f32[2048]{0:T(1024)}, u32[]{:S(2)}) copy-start(f32[2048]{0:T(1024)} %copy-done.44) | copy-start | bytes 24580
  (38 other events, 137.3 us)
Sparse Core Ops, SparseCore 0:
  413.4 238.0 all-reduce.11
where the time goes:
time: 678 us; the launch traced here: 669 us
  local copies, waits for them, and re-layouts  207 us (31%)
  matrix products  170 us (25%)
  waiting for transfers between devices  147 us (22%)
  other arithmetic  65.9 us (10%)
  blocking collectives  45.5 us (7%)
  starting transfers between devices  18.5 us (3%)
  between operations  15.5 us (2%)
    psum x1, waiting for transfers between devices, local(): lax.psum((grad_qkv, grad_out_w, grad_gain_attn, grad_bias_attn, grad_up,...  147 us
    psum x1, blocking collectives, local(): lax.psum((grad_qkv, grad_out_w, grad_gain_attn, grad_bias_attn, grad_up,...  45.5 us
    unnamed x130, local copies, waits for them, and re-layouts  44.2 us
    dot_general x1, matrix products, local(): hidden = jnp.dot(normed_two, w_up, preferred_element_type=jnp.float32)  44 us
    dot_general x5, matrix products, times_t(): lax.dot_general(first_op, second_op, (((1,), (1,)), ((), ())), preferred_...  42.5 us
    concatenate x2, local copies, waits for them, and re-layouts, local(): jnp.concatenate([jnp.zeros((2, pair_width), jnp.bfloat16), left_kv, keyva...  41.8 us
    dot_general x5, matrix products, inner_rows(): lax.dot_general(first_op, second_op, (((0,), (0,)), ((), ())), preferred_...  24.2 us
    ppermute x6, starting transfers between devices, from_behind(): lax.ppermute(value, axis, [(source, source + steps) for source in range(i...  18.4 us
  transfers between devices with their start and end apart: 7, of which 2 were waited for; matrix products, arithmetic and copies ran while one was open for 17% of the time, Pallas kernels for 0%

commit v1 on v0

v1 whole, which is shorter than its diff:
```python
import functools

import jax
import jax.numpy as jnp
from jax import lax
from jax.experimental import pallas as pl
from jax.experimental.pallas import tpu as pltpu
from jax.sharding import PartitionSpec as P

HEAD_DIM = 64
SEG = 16
GROUP = 64
KEYS = 128
MEMROWS = 16
FRONT = 32
EPS = 1e-05
FFC = 512
bf = jnp.bfloat16
f32 = jnp.float32
MESH = pl.DeviceIdType.MESH


def nn(a, b):
    return jnp.dot(a, b, preferred_element_type=f32)


def nt(a, b):
    return lax.dot_general(a, b, (((1,), (1,)), ((), ())), preferred_element_type=f32)


def tn(a, b):
    return lax.dot_general(a, b, (((0,), (0,)), ((), ())), preferred_element_type=f32)


def iota(shape, dim):
    return lax.broadcasted_iota(jnp.int32, shape, dim)


def standardise(x):
    mu = jnp.mean(x, axis=-1, keepdims=True)
    xc = x - mu
    rstd = lax.rsqrt(jnp.mean(xc * xc, axis=-1, keepdims=True) + EPS)
    return xc * rstd, rstd


def norm_grad(d, xhat, rstd, gain):
    g = d * gain
    return rstd * (
        g
        - jnp.mean(g, axis=-1, keepdims=True)
        - xhat * jnp.mean(g * xhat, axis=-1, keepdims=True)
    )


def rows_of(start, size, step=16):
    return pl.ds(pl.multiple_of(start, step), size)


def spread_heads(x):
    lane = iota((1, 256), 1) // HEAD_DIM
    return jnp.concatenate(
        [jnp.where(lane == h, x, jnp.zeros_like(x)) for h in range(4)], axis=0
    )


def own_columns(a):
    return jnp.where(iota((1, 128), 1) < HEAD_DIM, a[:GROUP], a[GROUP:])


def body(ntm, dims, *refs):
    T, D, FF, NU = dims
    NG = T // GROUP
    NS = T // SEG
    (
        frames_h, lens, wqkv, wo, wu, wd, ga, ba, gf, bfn, dy,
        out_h, gframes_h, units_h, small_h,
        X, Q, KV, MW, NT_, SUMM, ATTT, PR, MID, N2, N2T, DYT, OUT, D2, ACT, DH,
        MKV, SEL, KR, LO, HI, ST, EN, HX, HRL, HRR, HRM, SNL, SNR, U, UQ, SMALL, DSUM, DMK,
        lsem, osem, ssem, rsem,
    ) = refs
    TT = 256
    me = lax.axis_index("tm")
    right = lax.rem(me + 1, ntm)
    left = lax.rem(me + ntm - 1, ntm)

    load_x = pltpu.make_async_copy(frames_h, X, lsem.at[0])
    load_x.start()

    barrier = pltpu.get_barrier_semaphore()
    for other in (left, right):
        pl.semaphore_signal(barrier, inc=1, device_id={"tm": other}, device_id_type=MESH)
    pl.semaphore_wait(barrier, 2)

    def remote(k, src, dst, to):
        return pltpu.make_async_remote_copy(
            src_ref=src, dst_ref=dst, send_sem=ssem.at[k], recv_sem=rsem.at[k],
            device_id={"tm": to}, device_id_type=MESH,
        )

    to_right = remote(0, frames_h.at[T - 64 : T], HX.at[0:64], right)
    to_left = remote(1, frames_h.at[0:16], HX.at[64:80], left)
    to_right.start()
    to_left.start()

    for b in range(NU // 128):
        u = iota((128, 128), 0) + 128 * b
        first = jnp.zeros((128, 1), f32)
        last = jnp.zeros((128, 1), f32)
        for c in range(NU // 128):
            v = iota((128, 128), 1) + 128 * c
            n = lens[:, 128 * c : 128 * c + 128].astype(f32)
            first = first + jnp.sum(jnp.where(v < u, n, 0.0), axis=1, keepdims=True)
            last = last + jnp.sum(jnp.where(v <= u, n, 0.0), axis=1, keepdims=True)
        ST[128 * b : 128 * b + 128, :] = jnp.broadcast_to(first, (128, 128))
        EN[128 * b : 128 * b + 128, :] = jnp.broadcast_to(last, (128, 128))
    row = iota((KEYS, 128), 0)
    seg_q = (iota((KEYS, 128), 1) % GROUP) // SEG
    pos = row - MEMROWS
    mem_ok = (row < 8) & (seg_q <= row) & (row <= seg_q + 3)
    near_ok = (pos >= SEG * seg_q + 2) & (pos < SEG * seg_q + 52)
    rel = jnp.where(row < MEMROWS, row - 4, jnp.right_shift(pos, 4) - 2)
    KR[...] = jnp.where(
        jnp.where(row < MEMROWS, mem_ok.astype(jnp.int32), near_ok.astype(jnp.int32)) > 0,
        rel.astype(f32), -1e9,
    )

    def bounds(g, _):
        base = (me * NS + 4 * g).astype(f32)
        seg = base + ((iota((1, 128), 1) % GROUP) // SEG).astype(f32)
        st, en = ST[...], EN[...]
        lo = jnp.max(jnp.where(st <= seg, st, -1.0), axis=0, keepdims=True) - base
        hi = jnp.min(jnp.where(en > seg, en, 1e9), axis=0, keepdims=True) - base
        LO[g] = jnp.broadcast_to(lo, (8, 128))
        HI[g] = jnp.broadcast_to(hi, (8, 128))
        return 0

    lax.fori_loop(0, NG, bounds, 0)
    r512, c256 = iota((NG * 16, 256), 0), iota((NG * 16, 256), 1)
    seg = 4 * jnp.right_shift(r512, 4) - 4 + (r512 & 15)
    src = jnp.where(seg < 0, seg + 4 + NS, seg)
    SEL[...] = jnp.where(((r512 & 15) < 8) & (src == c256), 1.0, 0.0).astype(bf)

    load_x.wait()

    gain1, bias1 = ga[...], ba[...]
    mean16 = jnp.where(
        iota((16, TT), 0) == jnp.right_shift(iota((16, TT), 1), 4), 1.0 / SEG, 0.0
    ).astype(bf)

    def project(i, _):
        r = rows_of(i * TT, TT)
        xhat, _r = standardise(X[r, :].astype(f32))
        nb = (xhat * gain1 + bias1).astype(bf)
        NT_[:, rows_of(i * TT, TT, 128)] = nb.T
        SUMM[rows_of(i * 16, 16), :] = nn(mean16, nb).astype(bf)
        Q[r, :] = (nn(nb, wqkv[:, :D]) * HEAD_DIM**-0.5).astype(bf)
        KV[rows_of(i * TT + FRONT, TT), :] = nn(nb, wqkv[:, D:]).astype(bf)
        DYT[:, rows_of(i * TT, TT, 128)] = dy[r, :].T
        return 0

    lax.fori_loop(0, T // TT, project, 0)

    to_right.wait()
    to_left.wait()
    xhat, _r = standardise(HX[...].astype(f32))
    nb = (xhat * gain1 + bias1).astype(bf)
    edge = nn(nb, wqkv[:, D:]).astype(bf)
    KV[0:FRONT, :] = edge[32:64]
    KV[T + FRONT : T + FRONT + 16, :] = edge[64:80]
    SUMM[NS:256, :] = jnp.zeros((256 - NS, D), bf)
    SUMM[NS : NS + 16, :] = nn(mean16[:, :64], nb[:64]).astype(bf)
    MKV[...] = nn(SUMM[...], wqkv[:, D:]).astype(bf)
    MW[...] = nn(SEL[...], MKV[...]).astype(bf)

    gain2, bias2 = gf[...], bfn[...]

    def attend(i, _):
        r = rows_of(i * TT, TT)
        tiles = []
        for j in range(TT // GROUP):
            g = i * (TT // GROUP) + j
            win = rows_of(g * GROUP, 112)
            mem = rows_of(g * MEMROWS, MEMROWS)
            lo, hi = LO[g][0:1], HI[g][0:1]
            kr = KR[...]
            ok = (kr >= lo) & (kr < hi)
            cols = []
            for h in range(2):
                c = slice(256 * h, 256 * h + 256)
                cv = slice(D + 256 * h, D + 256 * h + 256)
                k4 = jnp.concatenate([MW[mem, c], KV[win, c]], axis=0)
                v4 = jnp.concatenate([MW[mem, cv], KV[win, cv]], axis=0)
                q4 = spread_heads(Q[rows_of(g * GROUP, GROUP), c])
                s = nt(k4, q4)
                for p in range(2):
                    cp = slice(128 * p, 128 * p + 128)
                    sp = jnp.where(ok, s[:, cp], -1e30)
                    e = jnp.exp(sp - jnp.max(sp, axis=0, keepdims=True))
                    pr = (e * (1.0 / jnp.sum(e, axis=0, keepdims=True))).astype(bf)
                    PR[rows_of(g * KEYS, KEYS), 256 * h + 128 * p : 256 * h + 128 * p + 128] = pr
                    cols.append(own_columns(tn(pr, v4[:, cp])))
            tiles.append(jnp.concatenate(cols, axis=1))
        att = jnp.concatenate(tiles, axis=0).astype(bf)
        ATTT[:, rows_of(i * TT, TT, 128)] = att.T
        mid = X[r, :].astype(f32) + nn(att, wo[...])
        MID[r, :] = mid
        xhat, _r = standardise(mid)
        n2 = (xhat * gain2 + bias2).astype(bf)
        N2[r, :] = n2
        N2T[:, rows_of(i * TT, TT, 128)] = n2.T
        return 0

    lax.fori_loop(0, T // TT, attend, 0)

    FT = 512
    for c in range(FF // FFC):
        cs = slice(c * FFC, (c + 1) * FFC)

        def ffn(i, _, c=c, cs=cs):
            r = rows_of(i * FT, FT)
            h = nn(N2[r, :], wu[:, cs])
            da = nt(dy[r, :], wd[cs, :])
            phi = 0.5 + 0.5 * lax.erf(h * 0.7071067811865476)
            slope = phi + h * (jnp.exp(h * h * -0.5) * 0.3989422804014327)
            a = (h * phi).astype(bf)
            d = (da * slope).astype(bf)
            ACT[r, :] = a
            DH[r, :] = d
            o = nn(a, wd[cs, :])
            d2 = nt(d, wu[:, cs])
            if c == 0:
                OUT[r, :] = MID[r, :] + o
                D2[r, :] = d2
            elif c < FF // FFC - 1:
                OUT[r, :] += o
                D2[r, :] += d2
            else:
                N2[r, :] = (OUT[r, :] + o).astype(bf)
                D2[r, :] += d2
            return 0

        lax.fori_loop(0, T // FT, ffn, 0)
        U[c] = nn(DYT[...], ACT[...]).astype(bf)
        U[FF // FFC + c] = nn(N2T[...], DH[...]).astype(bf)

    store_out = pltpu.make_async_copy(N2, out_h, osem.at[0])
    store_out.start()

    SMALL[...] = jnp.zeros_like(SMALL)

    def back_mid(i, _):
        r = rows_of(i * TT, TT)
        d2 = D2[r, :]
        xhat, rstd = standardise(MID[r, :])
        SMALL[2:3, :] += jnp.sum(d2 * xhat, axis=0, keepdims=True)
        SMALL[3:4, :] += jnp.sum(d2, axis=0, keepdims=True)
        dmid = dy[r, :].astype(f32) + norm_grad(d2, xhat, rstd, gain2)
        D2[r, :] = dmid
        db = dmid.astype(bf)
        ACT[r, :] = db
        DH[r, :] = nt(db, wo[...]).astype(bf)
        return 0

    lax.fori_loop(0, T // TT, back_mid, 0)
    U[2 * (FF // FFC)] = nn(ATTT[...], ACT[...]).astype(bf)

    for h in range(2):
        c = slice(256 * h, 256 * h + 256)
        cv = slice(D + 256 * h, D + 256 * h + 256)
        OUT[...] = jnp.zeros_like(OUT)

        def back_att(i, _, c=c, cv=cv):
            for j in range(4):
                g = lax.rem(i * 4 + j + NG - 1, NG)
                win = rows_of(g * GROUP, 112)
                mem = rows_of(g * MEMROWS, MEMROWS)
                qr = rows_of(g * GROUP, GROUP)
                k4 = jnp.concatenate([MW[mem, c], KV[win, c]], axis=0)
                v4 = jnp.concatenate([MW[mem, cv], KV[win, cv]], axis=0)
                q4 = spread_heads(Q[qr, c])
                o4 = spread_heads(DH[qr, c])
                pb = PR[rows_of(g * KEYS, KEYS), c]
                pf = pb.astype(f32)
                dp = nt(v4, o4)
                ds = (pf * (dp - jnp.sum(pf * dp, axis=0, keepdims=True))).astype(bf)
                dk = nn(ds, q4)
                dv = nn(pb, o4)
                dq = jnp.concatenate(
                    [
                        own_columns(tn(ds[:, 128 * p : 128 * p + 128], k4[:, 128 * p : 128 * p + 128]))
                        for p in range(2)
                    ],
                    axis=1,
                )
                Q[qr, c] = (dq * HEAD_DIM**-0.5).astype(bf)
                MW[mem, c] = dk[:MEMROWS].astype(bf)
                MW[mem, cv] = dv[:MEMROWS].astype(bf)
                OUT[win, 0:256] += dk[MEMROWS:]
                OUT[win, 256:512] += dv[MEMROWS:]
            return 0

        lax.fori_loop(0, NG // 4, back_att, 0)
        SNL[h, 0:FRONT, :] = OUT[0:FRONT, :].astype(bf)
        SNL[h, FRONT : FRONT + 16, 0:256] = MW[0:16, c]
        SNL[h, FRONT : FRONT + 16, 256:512] = MW[0:16, cv]
        SNR[h] = OUT[T + FRONT : T + FRONT + 16, :].astype(bf)
        give_left = remote(2 + 2 * h, SNL.at[h], HRL.at[h], left)
        give_right = remote(3 + 2 * h, SNR.at[h], HRR.at[h], right)
        give_left.start()
        give_right.start()
        give_left.wait()
        give_right.wait()
        live_l = jnp.where(me < ntm - 1, 1.0, 0.0).astype(f32)
        live_r = jnp.where(me > 0, 1.0, 0.0).astype(f32)
        OUT[T : T + FRONT, :] += HRL[h, 0:FRONT, :].astype(f32) * live_l
        OUT[FRONT : FRONT + 16, :] += HRR[h].astype(f32) * live_r
        pick = jnp.where(
            (iota((NS, 16), 0) == iota((NS, 16), 1) + NS - 4) & (iota((NS, 16), 1) < 4), 1.0, 0.0
        ).astype(bf)
        sel_own = SEL[:, 0:NS]
        dmw = jnp.concatenate([MW[:, c], MW[:, cv]], axis=1)
        dmk = tn(sel_own, dmw) + nn(pick, HRL[h, FRONT : FRONT + 16, :]) * live_l
        DMK[...] = dmk.astype(bf)

        def to_low(i, _, c=c, cv=cv):
            r = rows_of(i * TT + FRONT, TT)
            KV[r, c] = OUT[r, 0:256].astype(bf)
            KV[r, cv] = OUT[r, 256:512].astype(bf)
            return 0

        lax.fori_loop(0, T // TT, to_low, 0)
        own = slice(FRONT, T + FRONT)
        UQ[h, 0] = nn(NT_[...], Q[:, c]).astype(bf)
        UQ[h, 1] = (nn(NT_[...], KV[own, c]) + tn(SUMM[0:NS, :], DMK[:, 0:256])).astype(bf)
        UQ[h, 2] = (nn(NT_[...], KV[own, cv]) + tn(SUMM[0:NS, :], DMK[:, 256:512])).astype(bf)
        wk = slice(D + 256 * h, D + 256 * h + 256)
        wv = slice(2 * D + 256 * h, 2 * D + 256 * h + 256)
        dsum = (nt(DMK[:, 0:256], wqkv[:, wk]) + nt(DMK[:, 256:512], wqkv[:, wv])) * (1.0 / SEG)
        if h == 0:
            DSUM[...] = dsum
        else:
            DSUM[...] += dsum
        widen = jnp.where(
            jnp.right_shift(iota((TT, 16), 0), 4) == iota((TT, 16), 1), 1.0, 0.0
        ).astype(bf)

        def back_in(i, _, h=h, c=c, cv=cv, wk=wk, wv=wv):
            r = rows_of(i * TT, TT)
            rk = rows_of(i * TT + FRONT, TT)
            dn = nt(Q[r, c], wqkv[:, c]) + nt(KV[rk, c], wqkv[:, wk]) + nt(KV[rk, cv], wqkv[:, wv])
            if h == 0:
                MID[r, :] = dn
                return 0
            dn = dn + MID[r, :] + nn(widen, DSUM[rows_of(i * 16, 16), :].astype(bf))
            xhat, rstd = standardise(X[r, :].astype(f32))
            SMALL[0:1, :] += jnp.sum(dn * xhat, axis=0, keepdims=True)
            SMALL[1:2, :] += jnp.sum(dn, axis=0, keepdims=True)
            D2[r, :] += norm_grad(dn, xhat, rstd, gain1)
            return 0

        lax.fori_loop(0, T // TT, back_in, 0)

    store_g = pltpu.make_async_copy(D2, gframes_h, osem.at[1])
    store_g.start()
    nu = 2 * (FF // FFC) + 1
    store_u = pltpu.make_async_copy(U, units_h.at[0:nu], osem.at[2])
    store_u.start()
    store_q = [
        pltpu.make_async_copy(UQ.at[h, k], units_h.at[nu + k, :, pl.ds(256 * h, 256)], osem.at[4 + 3 * h + k])
        for h in range(2)
        for k in range(3)
    ]
    for s in store_q:
        s.start()
    store_s = pltpu.make_async_copy(SMALL, small_h, osem.at[3])
    store_s.start()
    store_out.wait()
    store_g.wait()
    store_u.wait()
    for s in store_q:
        s.wait()
    store_s.wait()


def local(frames, lens, wqkv, wo, wu, wd, ga, ba, gf, bfn, dy):
    T, D = frames.shape[1:]
    FF = wu.shape[1]
    NU = lens.shape[1]
    NG, NS = T // GROUP, T // SEG
    ntm = lax.axis_size("tm")
    nu = 2 * (FF // FFC) + 1
    V = pl.BlockSpec(memory_space=pltpu.VMEM)
    A = pl.BlockSpec(memory_space=pl.ANY)
    vm = lambda *s: pltpu.VMEM(s[:-1], s[-1])
    scratch = [
        vm(T, D, bf), vm(T, D, bf), vm(T + FRONT + 16, 2 * D, bf), vm(NG * 16, 2 * D, bf),
        vm(D, T, bf), vm(256, D, bf), vm(D, T, bf), vm(NG * KEYS, D, bf),
        vm(T, D, f32), vm(T, D, bf), vm(D, T, bf), vm(D, T, bf),
        vm(T + FRONT + 16, D, f32), vm(T, D, f32), vm(T, FFC, bf), vm(T, FFC, bf),
        vm(256, 2 * D, bf), vm(NG * 16, 256, bf), vm(KEYS, 128, f32), vm(NG, 8, 128, f32),
        vm(NG, 8, 128, f32), vm(NU, 128, f32), vm(NU, 128, f32), vm(80, D, bf),
        vm(2, 48, D, bf), vm(2, 16, D, bf), vm(2, 16, D, bf), vm(2, 48, D, bf), vm(2, 16, D, bf),
        vm(nu, D, D, bf), vm(2, 3, D, 256, bf), vm(8, D, f32), vm(NS, D, f32), vm(NS, D, bf),
        pltpu.SemaphoreType.DMA((2,)), pltpu.SemaphoreType.DMA((10,)),
        pltpu.SemaphoreType.DMA((6,)), pltpu.SemaphoreType.DMA((6,)),
    ]
    row = lambda v: v.reshape(1, D)
    out, gframes, units, small = pl.pallas_call(
        functools.partial(body, ntm, (T, D, FF, NU)),
        out_shape=[
            jax.ShapeDtypeStruct((T, D), bf),
            jax.ShapeDtypeStruct((T, D), f32),
            jax.ShapeDtypeStruct((nu + 3, D, D), bf),
            jax.ShapeDtypeStruct((8, D), f32),
        ],
        in_specs=[A] + [V] * 10,
        out_specs=[A] * 4,
        scratch_shapes=scratch,
        compiler_params=pltpu.CompilerParams(
            vmem_limit_bytes=60 * 2**20, collective_id=0, has_side_effects=True
        ),
    )(frames[0], lens, wqkv, wo, wu, wd, row(ga), row(ba), row(gf), row(bfn), dy[0])
    units = lax.psum(units, ("tm", "rows")).astype(f32)
    small = lax.psum(small, ("tm", "rows"))
    n = FF // FFC
    return (
        out[None],
        gframes[None],
        units[nu:].transpose(1, 0, 2).reshape(D, 3 * D),
        units[2 * n],
        units[n : 2 * n].transpose(1, 0, 2).reshape(D, FF),
        units[:n].transpose(0, 2, 1).reshape(FF, D),
        small[0], small[1], small[2], small[3],
    )


def solution(mesh):
    big, rep = P("rows", "tm", None), P()
    return jax.shard_map(
        local,
        mesh=mesh,
        in_specs=(big, P("rows", None)) + (rep,) * 8 + (big,),
        out_specs=(big, big) + (rep,) * 8,
        check_vma=False,
    )
```

time: 678 us -> 332 us (0.49); the launches traced: 669 us -> 332 us
  local copies, waits for them, and re-layouts: 207 us -> 33.8 us
  matrix products: 170 us -> 0 us
  Pallas kernels: 0 us -> 127 us
  other arithmetic: 65.9 us -> 4.51 us
  waiting for transfers between devices: 147 us -> 114 us
  starting transfers between devices: 18.5 us -> 0.04 us
  blocking collectives: 45.5 us -> 38.5 us
    dot_general x21 -> x0, matrix products: 170 us -> none  [the longest x1 44 us: local(): hidden = jnp.dot(normed_two, w_up, preferred_element_type=jnp.float32)]
    pallas_call x0 -> x1, Pallas kernels: none -> 127 us  [local(): pl.pallas_call(functools.partial(body, ntm, (T, D, FF, NU)), out_shape=[j...]
    reshape x6 -> x0, local copies, waits for them, and re-layouts: 41.9 us -> none  [the longest x2 13.1 us: local(): query_heads = queries.reshape(groups, 64, HEADS, HEAD_DIM)]
    concatenate x2 -> x0, local copies, waits for them, and re-layouts: 41.8 us -> none  [local(): jnp.concatenate([jnp.zeros((2, pair_width), jnp.bfloat16), left_kv, keyva...]
    slice x23 -> x1, local copies, waits for them, and re-layouts: 34.3 us -> 0.59 us  [local(): small[3]]
    psum x1, waiting for transfers between devices: 147 us -> 114 us  [local(): units = lax.psum(units, ('tm', 'rows')).astype(f32)]
    convert_element_type x6 -> x0, local copies, waits for them, and re-layouts: 31 us -> none  [the longest x2 13.5 us: local(): attn_low = attended.reshape(frame_count, model_width).astype(jnp.bfloat16)]
    unnamed x130 -> x10, local copies, waits for them, and re-layouts: 44.2 us -> 14.7 us
  transfers between devices with their start and end apart: 7 -> 1, of which waited for: 2 -> 1; matrix products, arithmetic and copies ran while one was open for 17% -> 0% of each run, Pallas kernels for 0% -> 0%
where the time goes in v1:
time: 332 us
  Pallas kernels  127 us (38%)
  waiting for transfers between devices  114 us (34%)
  blocking collectives  38.5 us (12%)
  local copies, waits for them, and re-layouts  33.8 us (10%)
  between operations  14.1 us (4%)
  other arithmetic  4.51 us (1%)
    pallas_call x1, Pallas kernels, local(): pl.pallas_call(functools.partial(body, ntm, (T, D, FF, NU)), out_shape=[j...  127 us
    psum x1, waiting for transfers between devices, local(): units = lax.psum(units, ('tm', 'rows')).astype(f32)  114 us
    psum x1, blocking collectives, local(): small = lax.psum(small, ('tm', 'rows'))  38.5 us
    unnamed x10, local copies, waits for them, and re-layouts  14.7 us
    transpose x2, local copies, waits for them, and re-layouts, local(): units[:n].transpose(0, 2, 1).reshape(FF, D)  9.59 us
  transfers between devices with their start and end apart: 1, of which 1 were waited for; matrix products, arithmetic and copies ran while one was open for 0% of the time, Pallas kernels for 0%

profile of v1, /device:TPU:0, one launch (start us, length us, event | category | flops | bytes accessed | tf_op | source)
XLA Modules:
  0.0 331.9 jit_solution(9568355114770619379)
XLA Ops:
  7.2 0.0 all-reduce.2.cloned.1.call-start
  7.2 127.1 %shard_map.186 = (bf16[2048,512]{1,0:T(8,128)(2,1)}, f32[2048,512]{1,0:T(8,128)}, bf16[12,512,512]{2,1,0:T(8,128)(2,1)}, f32[8,512]{1,0:T(8,128)}) custom-call(bf16[2048,512]{1,0:T(8,128)(2,1)} %bitcast.28, s32[1,128]{1,0:T(1,128)} %refs_1_.1, bf16[512,1536]{1,0:T(8,128)(2,1)} %refs_2_.1, bf16[512,512]{1,0:T(8,128)(2,1)} %refs_3_.1, ...), custom_call_target="tpu_custom_call" | custom-call | tf_op jit(solution)/shard_map/pallas_call | solution.py:408
  134.3 0.0 copy-start.2
  134.3 0.0 all-reduce.2.cloned.1.call-update
  134.4 0.7 copy-done.2
  135.1 38.5 %psum.15 = f32[8,512]{1,0:T(8,128)S(1)} all-reduce(f32[8,512]{1,0:T(8,128)S(1)} %copy-done.2), channel_id=1, replica_groups=mesh['tm'=16,'rows'=2] {'tm','rows'}, use_global_device_ids=true, to_apply=%region_1.0 | all-reduce | flops 4096 | bytes 32768 | tf_op jit(solution)/shard_map/psum | solution.py:424
  173.6 0.6 fusion
  174.2 113.9 %all-reduce.2.cloned.1.call-done = bf16[12,512,512]{2,1,0:T(8,128)(2,1)} async-done(((bf16[12,512,512]{2,1,0:T(8,128)(2,1)}), bf16[12,512,512]{2,1,0:T(8,128)(2,1)}) %all-reduce.2.cloned.1.call-update) | async-done | bytes 6291472 | tf_op jit(solution)/shard_map/psum | solution.py:423
  288.1 4.5 %convert_element_type.3 = f32[12,512,512]{2,1,0:T(8,128)S(1)} convert(bf16[12,512,512]{2,1,0:T(8,128)(2,1)} %all-reduce.2.cloned.1.call-done) | non-fusion elementwise | flops 3145728 | bytes 18874368 | tf_op jit(solution)/shard_map/convert_element_type | solution.py:423
  292.6 1.0 slice_bitcast_fusion.3
  293.6 0.3 slice_bitcast_fusion.2
  293.9 4.4 %slice_bitcast_fusion = (f32[4,512,512]{1,2,0:T(8,128)}, f32[512,4,512]{2,0,1:T(8,128)}) fusion(f32[12,512,512]{2,1,0:T(8,128)S(1)} %convert_element_type.3), kind=kLoop, calls=%fused_computation | loop fusion | bytes 16777216 | tf_op jit(solution)/shard_map/transpose | solution.py:432
  298.3 5.2 %copy.23 = f32[4,512,512]{2,1,0:T(8,128)} copy(f32[4,512,512]{1,2,0:T(8,128)} %get-tuple-element.28) | data formatting | bytes 8388608 | tf_op jit(solution)/shard_map/transpose | solution.py:432
  303.5 2.4 copy.21
  305.9 3.5 %copy.24 = f32[512,1536]{1,0:T(8,128)} copy(f32[512,1536]{0,1:T(8,128)} %bitcast.24) | data formatting | bytes 6291456
  309.4 5.2 %copy.22 = f32[512,4,512]{0,2,1:T(8,128)} copy(f32[512,4,512]{2,0,1:T(8,128)} %get-tuple-element.29) | data formatting | bytes 8388608 | tf_op jit(solution)/shard_map/transpose | solution.py:431
  314.6 0.0 copy-start.1
  314.6 5.5 %copy.25 = f32[512,2048]{1,0:T(8,128)} copy(f32[512,2048]{0,1:T(8,128)} %bitcast.23) | data formatting | bytes 8388608
  320.1 0.0 copy-start
  320.1 0.0 copy-done.1
  320.1 1.3 copy.29
  321.5 1.6 copy-done
  323.1 2.0 copy.30
Async XLA Ops:
  7.2 280.9 %all-reduce.2.cloned.1.call-start = ((), (), s32[]{:S(2)}) async-start(), calls=%async_computation | async-start | bytes 12582912 | tf_op jit(solution)/shard_map/psum | solution.py:423
  134.3 0.7 copy-start.2
  314.6 5.5 %copy-start.1 = (bf16[2048,512]{1,0:T(8,128)(2,1)S(1)}, bf16[2048,512]{1,0:T(8,128)(2,1)}, u32[]{:S(2)}) copy-start(bf16[2048,512]{1,0:T(8,128)(2,1)} %get-tuple-element.14) | copy-start | bytes 6291460
  320.1 2.9 copy-start
Sparse Core Ops, SparseCore 0:
  134.5 153.5 all-reduce.1

commit v2 on v1

v2 whole, which is shorter than its diff:
```python
import functools

import jax
import jax.numpy as jnp
from jax import lax
from jax.experimental import pallas as pl
from jax.experimental.pallas import tpu as pltpu
from jax.sharding import PartitionSpec as P

HEAD_DIM = 64
SEG = 16
GROUP = 64
KEYS = 128
MEMROWS = 16
FRONT = 32
EPS = 1e-05
FFC = 512
TT = 512
GI = TT // GROUP
bf = jnp.bfloat16
f32 = jnp.float32
MESH = pl.DeviceIdType.MESH
ORDER = "10031110qqq"
GAPS = {
    "0": [1, 5, 4, 3, 3, 3, 3, 4, 5, 1],
    "q": [1, 5, 4, 4, 5, 1],
}


def nn(a, b):
    return jnp.dot(a, b, preferred_element_type=f32)


def nt(a, b):
    return lax.dot_general(a, b, (((1,), (1,)), ((), ())), preferred_element_type=f32)


def tn(a, b):
    return lax.dot_general(a, b, (((0,), (0,)), ((), ())), preferred_element_type=f32)


def iota(shape, dim):
    return lax.broadcasted_iota(jnp.int32, shape, dim)


def standardise(x):
    mu = jnp.mean(x, axis=-1, keepdims=True)
    xc = x - mu
    rstd = lax.rsqrt(jnp.mean(xc * xc, axis=-1, keepdims=True) + EPS)
    return xc * rstd, rstd


def norm_grad(d, xhat, rstd, gain):
    g = d * gain
    return rstd * (
        g
        - jnp.mean(g, axis=-1, keepdims=True)
        - xhat * jnp.mean(g * xhat, axis=-1, keepdims=True)
    )


def rows_of(start, size, step=16):
    return pl.ds(pl.multiple_of(start, step), size)


def spread_heads(x):
    lane = iota((1, 256), 1) // HEAD_DIM
    return jnp.concatenate(
        [jnp.where(lane == h, x, jnp.zeros_like(x)) for h in range(4)], axis=0
    )


def own_columns(a):
    return jnp.where(iota((1, 128), 1) < HEAD_DIM, a[:GROUP], a[GROUP:])


class Reduction:
    def __init__(self, stages, rows, own, got, sems, gaps, name):
        self.own, self.got, self.name = own, got, name
        self.ssem, self.rsem, self.freed = sems
        self.gaps = gaps
        self.pos, self.rest = 0, 0
        self.levels = []
        lo, size, at, sem = 0, rows, 0, 0
        for axes in stages:
            k = len(axes)
            split = size % (16 << k) == 0
            part = size >> k if split else size
            rank = sum(bit * 2**j for j, (bit, _) in enumerate(axes))
            peers = []
            for m in range(1, 1 << k):
                flip = [(m >> j) & 1 for j in range(k)]
                other = sum(
                    (1 - bit if f else bit) * 2**j for j, (f, (bit, _)) in enumerate(zip(flip, axes))
                )
                dev = {}
                for f, (bit, (axis, here, step)) in zip(flip, axes):
                    if f:
                        dev[axis] = dev.get(axis, here) + (1 - 2 * bit) * step
                peers.append((dev, other))
            mine = lo + rank * part if split else lo
            self.levels.append((peers, lo, mine, part, at, sem, split))
            lo, size = mine, part
            at += part * len(peers)
            sem += 2 * len(peers)
        self.steps = [(i, True) for i in range(len(stages))]
        self.steps += [(i, False) for i in reversed(range(len(stages))) if self.levels[i][6]]

    @staticmethod
    def landing(stages, rows):
        size, at, sem = rows, 0, 0
        for k in stages:
            size = size >> k if size % (16 << k) == 0 else size
            at += size * ((1 << k) - 1)
            sem += 2 * ((1 << k) - 1)
        return at, sem

    def copies(self, k):
        i, inward = self.steps[k]
        peers, lo, mine, part, at, sem, split = self.levels[i]
        made = []
        for q, (dev, other) in enumerate(peers):
            if inward:
                src = self.own(lo + other * part if split else lo, part)
                dst = self.got(at + q * part, part)
            else:
                src = dst = self.own(mine, part)
            z = sem + 2 * q + (0 if inward else 1)
            made.append(
                pltpu.make_async_remote_copy(
                    src_ref=src, dst_ref=dst, send_sem=self.ssem.at[z], recv_sem=self.rsem.at[z],
                    device_id=dev, device_id_type=MESH,
                )
            )
        return made

    def finish(self, k):
        for copy in self.copies(k):
            copy.wait()
        i, inward = self.steps[k]
        if inward:
            peers, _, mine, part, at, _, split = self.levels[i]
            if split:
                for dev, _other in peers:
                    pl.semaphore_signal(
                        self.freed.at[i], inc=1, device_id=dev, device_id_type=MESH
                    )
            view = self.own(mine, part)
            total = view[...]
            for q in range(len(peers)):
                total = total + self.got(at + q * part, part)[...]
            view[...] = total

    def advance(self):
        if self.pos:
            self.finish(self.pos - 1)
        if self.pos < len(self.steps):
            i, inward = self.steps[self.pos]
            if not inward:
                pl.semaphore_wait(self.freed.at[i], len(self.levels[i][0]))
            for copy in self.copies(self.pos):
                copy.start()
            self.rest = self.gaps[min(self.pos, len(self.gaps) - 1)]
        self.pos += 1
        return self.pos > len(self.steps)


def schemes(bits):
    low, high = list(range(min(2, bits))), list(range(2, bits))
    one = lambda order: [[b] for b in order]
    return {
        "0": one(low + high),
        "1": one(low[::-1] + high),
        "2": one(high + low),
        "3": one(high + low[::-1]),
        "q": [low] + [high[i : i + 2] for i in range(0, len(high), 2)],
    }


def body(ntm, dims, *refs):
    T, D, FF, NU = dims
    NG = T // GROUP
    NS = T // SEG
    NC = FF // FFC
    nu = 2 * NC + 1
    (
        frames_h, dy_h, wqkv_h, wo_h, wu_h, wd_h, lens, ga, ba, gf, bfn,
        out_h, gframes_h, units_h, uqkv_h, small_h,
        X, DY, wqkv, wo, wu, wd,
        Q, KV, MW, NT_, SUMM, ATTT, PR, MID, N2, N2T, DYT, OUT, D2, ACT, DH,
        SEL, KR, LO, HI, HX, HRL, HRR, SNL, SNR, U, UR, UQR, SMALL, SMR, DSUM, DMK,
        lsem, osem, ssem, rsem, ussem, ursem, xssem, xrsem, freed,
    ) = refs
    me, row_id = lax.axis_index("tm"), lax.axis_index("rows")
    right = lax.rem(me + 1, ntm)
    left = lax.rem(me + ntm - 1, ntm)

    loads = [
        pltpu.make_async_copy(src, dst, lsem.at[k])
        for k, (src, dst) in enumerate(
            [(frames_h, X), (wqkv_h, wqkv), (dy_h, DY), (wo_h, wo), (wu_h, wu), (wd_h, wd)]
        )
    ]
    for load in loads:
        load.start()

    bits = ntm.bit_length() - 1
    axes = [(row_id, ("rows", row_id, 1))]
    for b in range(bits):
        axes.append((lax.rem(lax.div(me, 2**b), 2), ("tm", me, 2**b)))

    def flipped(which):
        dev = {}
        for bit, (axis, here, step) in which:
            dev[axis] = dev.get(axis, here) + (1 - 2 * bit) * step
        return dev

    barrier = pltpu.get_barrier_semaphore()
    others = [{"tm": left}, {"tm": right}] + [flipped([a]) for a in axes]
    low = axes[1:3]
    others += [flipped(low)] if len(low) == 2 else []
    others += [flipped(axes[i : i + 2]) for i in range(3, bits, 2)]
    for other in others:
        pl.semaphore_signal(barrier, inc=1, device_id=other, device_id_type=MESH)

    def remote(k, src, dst, to):
        return pltpu.make_async_remote_copy(
            src_ref=src, dst_ref=dst, send_sem=ssem.at[k], recv_sem=rsem.at[k],
            device_id={"tm": to}, device_id_type=MESH,
        )

    kinds = schemes(bits)
    active = []

    def reduction(k, kind, rows, own, got):
        stages = [[axes[0]]] + [[axes[1 + b] for b in stage] for stage in kinds[kind]]
        gaps = GAPS[kind] if kind in GAPS else GAPS["0"]
        active.append(Reduction(stages, rows, own, got, (ussem.at[k], ursem.at[k], freed.at[k]), gaps, k))

    def slot(every=False):
        for red in list(active):
            red.rest -= 1
            if (red.rest <= 0 or every) and red.advance():
                active.remove(red)

    def slots(i, count):
        for k in range(count):
            if active:

                @pl.when(i == k)
                def _():
                    slot()

    def reduce_unit(k, kind):
        reduction(
            k, kind, D,
            lambda lo, n: U.at[k, rows_of(lo, n)],
            lambda lo, n: UR.at[k, lo : lo + n],
        )

    for load in loads[:3]:
        load.wait()
    gain1, bias1 = ga[...], ba[...]
    NM = TT // SEG
    mean16 = jnp.where(
        iota((NM, TT), 0) == jnp.right_shift(iota((NM, TT), 1), 4), 1.0 / SEG, 0.0
    ).astype(bf)

    def project(i, _):
        r = rows_of(i * TT, TT)
        xhat, _r = standardise(X[r, :].astype(f32))
        nb = (xhat * gain1 + bias1).astype(bf)
        NT_[:, rows_of(i * TT, TT, 128)] = nb.T
        SUMM[rows_of(i * NM, NM), :] = nn(mean16, nb).astype(bf)
        Q[r, :] = (nn(nb, wqkv[:, :D]) * HEAD_DIM**-0.5).astype(bf)
        KV[rows_of(i * TT + FRONT, TT), :] = nn(nb, wqkv[:, D:]).astype(bf)
        DYT[:, rows_of(i * TT, TT, 128)] = DY[r, :].T
        return 0

    lax.fori_loop(0, T // TT, project, 0)

    pl.semaphore_wait(barrier, len(others))
    to_right = remote(0, frames_h.at[T - 64 : T], HX.at[0:64], right)
    to_left = remote(1, frames_h.at[0:16], HX.at[64:80], left)
    to_right.start()
    to_left.start()

    for b in range(NU // 128):
        u = iota((128, 128), 0) + 128 * b
        first = jnp.zeros((128, 1), f32)
        last = jnp.zeros((128, 1), f32)
        for c in range(NU // 128):
            v = iota((128, 128), 1) + 128 * c
            n = lens[:, 128 * c : 128 * c + 128].astype(f32)
            first = first + jnp.sum(jnp.where(v < u, n, 0.0), axis=1, keepdims=True)
            last = last + jnp.sum(jnp.where(v <= u, n, 0.0), axis=1, keepdims=True)
        MID[128 * b : 128 * b + 128, 0:128] = jnp.broadcast_to(first, (128, 128))
        MID[128 * b : 128 * b + 128, 128:256] = jnp.broadcast_to(last, (128, 128))
    row = iota((KEYS, 128), 0)
    seg_q = (iota((KEYS, 128), 1) % GROUP) // SEG
    pos = row - MEMROWS
    mem_ok = (row < 8) & (seg_q <= row) & (row <= seg_q + 3)
    near_ok = (pos >= SEG * seg_q + 2) & (pos < SEG * seg_q + 52)
    rel = jnp.where(row < MEMROWS, row - 4, jnp.right_shift(pos, 4) - 2)
    KR[...] = jnp.where(
        jnp.where(row < MEMROWS, mem_ok.astype(jnp.int32), near_ok.astype(jnp.int32)) > 0,
        rel.astype(f32), -1e9,
    )

    def bounds(g, _):
        base = (me * NS + 4 * g).astype(f32)
        seg = base + ((iota((1, 128), 1) % GROUP) // SEG).astype(f32)
        st, en = MID[0:NU, 0:128], MID[0:NU, 128:256]
        lo = jnp.max(jnp.where(st <= seg, st, -1.0), axis=0, keepdims=True) - base
        hi = jnp.min(jnp.where(en > seg, en, 1e9), axis=0, keepdims=True) - base
        LO[g] = jnp.broadcast_to(lo, (8, 128))
        HI[g] = jnp.broadcast_to(hi, (8, 128))
        return 0

    lax.fori_loop(0, NG, bounds, 0)
    r512, c256 = iota((NG * 16, 256), 0), iota((NG * 16, 256), 1)
    seg = 4 * jnp.right_shift(r512, 4) - 4 + (r512 & 15)
    src = jnp.where(seg < 0, seg + 4 + NS, seg)
    SEL[...] = jnp.where(((r512 & 15) < 8) & (src == c256), 1.0, 0.0).astype(bf)
    SMALL[...] = jnp.zeros_like(SMALL)

    to_right.wait()
    to_left.wait()
    xhat, _r = standardise(HX[...].astype(f32))
    nb = (xhat * gain1 + bias1).astype(bf)
    edge = nn(nb, wqkv[:, D:]).astype(bf)
    KV[0:FRONT, :] = edge[32:64]
    KV[T + FRONT : T + FRONT + 16, :] = edge[64:80]
    SUMM[NS:256, :] = jnp.zeros((256 - NS, D), bf)
    SUMM[NS : NS + 16, :] = nn(mean16[:16, :64], nb[:64]).astype(bf)
    MW[...] = nn(SEL[...], nn(SUMM[...], wqkv[:, D:]).astype(bf)).astype(bf)

    loads[3].wait()
    gain2, bias2 = gf[...], bfn[...]

    def window(g, c):
        win = rows_of(g * GROUP, 112)
        mem = rows_of(g * MEMROWS, MEMROWS)
        return jnp.concatenate([MW[mem, c], KV[win, c]], axis=0)

    def attend(i, _):
        r = rows_of(i * TT, TT)
        gs = [i * GI + j for j in range(GI)]
        for j, g in enumerate(gs):
            for h in range(2):
                c = slice(256 * h, 256 * h + 256)
                q4 = spread_heads(Q[rows_of(g * GROUP, GROUP), c])
                OUT[KEYS * j : KEYS * j + KEYS, c] = nt(window(g, c), q4)
        for j, g in enumerate(gs):
            lo, hi = LO[g][0:1], HI[g][0:1]
            kr = KR[...]
            ok = (kr >= lo) & (kr < hi)
            for p in range(D // 128):
                cp = slice(128 * p, 128 * p + 128)
                s = jnp.where(ok, OUT[KEYS * j : KEYS * j + KEYS, cp], -1e30)
                e = jnp.exp(s - jnp.max(s, axis=0, keepdims=True))
                pr = e * (1.0 / jnp.sum(e, axis=0, keepdims=True))
                PR[rows_of(g * KEYS, KEYS), cp] = pr.astype(bf)
        tiles = []
        for g in gs:
            cols = []
            for p in range(D // 128):
                cp = slice(128 * p, 128 * p + 128)
                v2 = window(g, slice(D + 128 * p, D + 128 * p + 128))
                cols.append(own_columns(tn(PR[rows_of(g * KEYS, KEYS), cp], v2)))
            tiles.append(jnp.concatenate(cols, axis=1))
        att = jnp.concatenate(tiles, axis=0).astype(bf)
        ATTT[:, rows_of(i * TT, TT, 128)] = att.T
        mid = X[r, :].astype(f32) + nn(att, wo[...])
        MID[r, :] = mid
        xhat, _r = standardise(mid)
        n2 = (xhat * gain2 + bias2).astype(bf)
        N2[r, :] = n2
        N2T[:, rows_of(i * TT, TT, 128)] = n2.T
        return 0

    lax.fori_loop(0, T // TT, attend, 0)

    loads[4].wait()
    loads[5].wait()
    for c in range(NC):
        cs = slice(c * FFC, (c + 1) * FFC)

        def ffn(i, _, c=c, cs=cs):
            slots(i, T // TT)

            r = rows_of(i * TT, TT)
            h = nn(N2[r, :], wu[:, cs])
            da = nt(DY[r, :], wd[cs, :])
            phi = 0.5 + 0.5 * lax.erf(h * 0.7071067811865476)
            slope = phi + h * (jnp.exp(h * h * -0.5) * 0.3989422804014327)
            a = (h * phi).astype(bf)
            d = (da * slope).astype(bf)
            ACT[r, :] = a
            DH[r, :] = d
            o = nn(a, wd[cs, :])
            d2 = nt(d, wu[:, cs])
            if c == 0:
                OUT[r, :] = MID[r, :] + o
                D2[r, :] = d2
            elif c < NC - 1:
                OUT[r, :] += o
                D2[r, :] += d2
            else:
                N2[r, :] = (OUT[r, :] + o).astype(bf)
                D2[r, :] += d2
            return 0

        lax.fori_loop(0, T // TT, ffn, 0)
        U[c] = nn(DYT[...], ACT[...]).astype(bf)
        reduce_unit(c, ORDER[2 * c])
        slot()
        U[NC + c] = nn(N2T[...], DH[...]).astype(bf)
        reduce_unit(NC + c, ORDER[2 * c + 1])
        slot()

    store_out = pltpu.make_async_copy(N2, out_h, osem.at[0])
    store_out.start()

    def back_mid(i, _):
        slots(i, T // TT)

        r = rows_of(i * TT, TT)
        d2 = D2[r, :]
        xhat, rstd = standardise(MID[r, :])
        SMALL[2:3, :] += jnp.sum(d2 * xhat, axis=0, keepdims=True)
        SMALL[3:4, :] += jnp.sum(d2, axis=0, keepdims=True)
        dmid = DY[r, :].astype(f32) + norm_grad(d2, xhat, rstd, gain2)
        D2[r, :] = dmid
        db = dmid.astype(bf)
        ACT[r, :] = db
        DH[r, :] = nt(db, wo[...]).astype(bf)
        return 0

    lax.fori_loop(0, T // TT, back_mid, 0)
    U[2 * NC] = nn(ATTT[...], ACT[...]).astype(bf)
    reduce_unit(2 * NC, ORDER[2 * NC])

    for h in range(2):
        c = slice(256 * h, 256 * h + 256)
        cv = slice(D + 256 * h, D + 256 * h + 256)
        OUT[...] = jnp.zeros_like(OUT)
        give_left = remote(2 + 2 * h, SNL.at[h], HRL.at[h], left)
        give_right = remote(3 + 2 * h, SNR.at[h], HRR.at[h], right)

        def back_att(i, _, h=h, c=c, cv=cv, give_left=give_left, give_right=give_right):
            slots(i, NG // GI)

            gs = [lax.rem(i * GI + j + NG - 1, NG) for j in range(GI)]
            half = slice(0, 256)
            for j, g in enumerate(gs):
                o4 = spread_heads(DH[rows_of(g * GROUP, GROUP), c])
                MID[GI * KEYS + KEYS * j : GI * KEYS + KEYS * j + KEYS, half] = nt(window(g, cv), o4)
            for j, g in enumerate(gs):
                for p in range(2):
                    cp = slice(128 * p, 128 * p + 128)
                    cg = slice(256 * h + 128 * p, 256 * h + 128 * p + 128)
                    pf = PR[rows_of(g * KEYS, KEYS), cg].astype(f32)
                    t = pf * MID[GI * KEYS + KEYS * j : GI * KEYS + KEYS * j + KEYS, cp]
                    ds = t - pf * jnp.sum(t, axis=0, keepdims=True)
                    ACT[KEYS * j : KEYS * j + KEYS, cp] = ds.astype(bf)
            for j, g in enumerate(gs):
                k4 = window(g, c)
                for p in range(2):
                    cp = slice(128 * p, 128 * p + 128)
                    dq = own_columns(tn(ACT[KEYS * j : KEYS * j + KEYS, cp], k4[:, cp]))
                    ACT[GROUP * j : GROUP * j + GROUP, 256 + 128 * p : 384 + 128 * p] = (
                        dq * HEAD_DIM**-0.5
                    ).astype(bf)
            for j, g in enumerate(gs):
                qr = rows_of(g * GROUP, GROUP)
                MID[KEYS * j : KEYS * j + KEYS, 0:256] = nn(
                    ACT[KEYS * j : KEYS * j + KEYS, half], spread_heads(Q[qr, c])
                )
                MID[KEYS * j : KEYS * j + KEYS, 256:512] = nn(
                    PR[rows_of(g * KEYS, KEYS), c], spread_heads(DH[qr, c])
                )
            for j, g in enumerate(gs):
                win = rows_of(g * GROUP, 112)
                mem = rows_of(g * MEMROWS, MEMROWS)
                Q[rows_of(g * GROUP, GROUP), c] = ACT[GROUP * j : GROUP * j + GROUP, 256:512]
                MW[mem, c] = MID[KEYS * j : KEYS * j + MEMROWS, 0:256].astype(bf)
                MW[mem, cv] = MID[KEYS * j : KEYS * j + MEMROWS, 256:512].astype(bf)
                OUT[win, :] += MID[KEYS * j + MEMROWS : KEYS * j + KEYS, :]

            @pl.when(i == 0)
            def _():
                SNL[h, 0:FRONT, :] = OUT[0:FRONT, :].astype(bf)
                SNL[h, FRONT : FRONT + 16, 0:256] = MW[0:16, c]
                SNL[h, FRONT : FRONT + 16, 256:512] = MW[0:16, cv]
                SNR[h] = OUT[T + FRONT : T + FRONT + 16, :].astype(bf)
                give_left.start()
                give_right.start()

            return 0

        lax.fori_loop(0, NG // GI, back_att, 0)
        give_left.wait()
        give_right.wait()
        live_l = jnp.where(me < ntm - 1, 1.0, 0.0).astype(f32)
        live_r = jnp.where(me > 0, 1.0, 0.0).astype(f32)
        OUT[T : T + FRONT, :] += HRL[h, 0:FRONT, :].astype(f32) * live_l
        OUT[FRONT : FRONT + 16, :] += HRR[h].astype(f32) * live_r
        pick = jnp.where(
            (iota((NS, 16), 0) == iota((NS, 16), 1) + NS - 4) & (iota((NS, 16), 1) < 4), 1.0, 0.0
        ).astype(bf)
        dmw = jnp.concatenate([MW[:, c], MW[:, cv]], axis=1)
        dmk = tn(SEL[:, 0:NS], dmw) + nn(pick, HRL[h, FRONT : FRONT + 16, :]) * live_l
        DMK[:, 512 * h : 512 * h + 512] = dmk.astype(bf)

        def to_low(i, _, c=c, cv=cv):
            r = rows_of(i * TT + FRONT, TT)
            KV[r, c] = OUT[r, 0:256].astype(bf)
            KV[r, cv] = OUT[r, 256:512].astype(bf)
            return 0

        lax.fori_loop(0, T // TT, to_low, 0)
        own = slice(FRONT, T + FRONT)
        at = 768 * h
        N2T[:, at : at + 256] = nn(NT_[...], Q[:, c]).astype(bf)
        N2T[:, at + 256 : at + 512] = (
            nn(NT_[...], KV[own, c]) + tn(SUMM[0:NS, :], DMK[:, 512 * h : 512 * h + 256])
        ).astype(bf)
        N2T[:, at + 512 : at + 768] = (
            nn(NT_[...], KV[own, cv]) + tn(SUMM[0:NS, :], DMK[:, 512 * h + 256 : 512 * h + 512])
        ).astype(bf)
        reduction(
            nu + h, ORDER[2 * NC + 1 + h], D,
            lambda lo, n, at=at: N2T.at[rows_of(lo, n), at : at + 768],
            lambda lo, n, h=h: UQR.at[h, lo : lo + n],
        )
        slot()

    dsum = jnp.zeros((NS, D), f32)
    for h in range(2):
        for k in range(2):
            lo = D * (1 + k) + 256 * h
            dsum += nt(DMK[:, 512 * h + 256 * k : 512 * h + 256 * k + 256], wqkv[:, lo : lo + 256])
    DSUM[...] = (dsum * (1.0 / SEG)).astype(bf)
    widen = jnp.where(
        jnp.right_shift(iota((TT, NM), 0), 4) == iota((TT, NM), 1), 1.0, 0.0
    ).astype(bf)

    def back_in(i, _):
        slots(i, T // TT)

        r = rows_of(i * TT, TT)
        rk = rows_of(i * TT + FRONT, TT)
        dn = nt(Q[r, :], wqkv[:, :D]) + nt(KV[rk, :], wqkv[:, D:])
        dn = dn + nn(widen, DSUM[rows_of(i * NM, NM), :])
        xhat, rstd = standardise(X[r, :].astype(f32))
        SMALL[0:1, :] += jnp.sum(dn * xhat, axis=0, keepdims=True)
        SMALL[1:2, :] += jnp.sum(dn, axis=0, keepdims=True)
        D2[r, :] += norm_grad(dn, xhat, rstd, gain1)
        return 0

    lax.fori_loop(0, T // TT, back_in, 0)
    store_g = pltpu.make_async_copy(D2, gframes_h, osem.at[1])
    store_g.start()

    def small_copy(k):
        return pltpu.make_async_remote_copy(
            src_ref=SMALL, dst_ref=SMR.at[k], send_sem=xssem.at[k], recv_sem=xrsem.at[k],
            device_id=flipped([axes[k]]), device_id_type=MESH,
        )

    for k in range(bits + 1):
        small_copy(k).start()
        slot(True)
        small_copy(k).wait()
        SMALL[...] += SMR[k]
    while active:
        slot(True)
    store_u = pltpu.make_async_copy(U, units_h, osem.at[2])
    store_q = pltpu.make_async_copy(N2T.at[:, 0 : 3 * D], uqkv_h, osem.at[3])
    store_s = pltpu.make_async_copy(SMALL, small_h, osem.at[4])
    for store in (store_u, store_q, store_s):
        store.start()
    for store in (store_out, store_g, store_u, store_q, store_s):
        store.wait()


def finish(gd, gu, go, gq, out, gframes, small, gd_o, gu_o, go_o, gq_o, out_o, gframes_o, *vectors):
    for k, vector in enumerate(vectors):
        vector[...] = small[k : k + 1, :]
    gd_o[...] = gd[0].astype(f32).T
    gu_o[...] = gu[0].astype(f32)
    go_o[...] = go[0].astype(f32)
    for h in range(2):
        for p in range(3):
            gq_o[:, 512 * p + 256 * h : 512 * p + 256 * h + 256] = gq[
                :, 768 * h + 256 * p : 768 * h + 256 * p + 256
            ].astype(f32)
    out_o[...] = out[...]
    gframes_o[...] = gframes[...]


def local(frames, lens, wqkv, wo, wu, wd, ga, ba, gf, bfn, dy):
    T, D = frames.shape[1:]
    FF = wu.shape[1]
    NU = lens.shape[1]
    NG, NS = T // GROUP, T // SEG
    NC = FF // FFC
    ntm = lax.axis_size("tm")
    levels = ntm.bit_length()
    nu = 2 * NC + 1
    V = pl.BlockSpec(memory_space=pltpu.VMEM)
    A = pl.BlockSpec(memory_space=pl.ANY)
    vm = lambda *s: pltpu.VMEM(s[:-1], s[-1])
    dma = lambda *s: pltpu.SemaphoreType.DMA(s)
    land, sems = 0, 0
    for kind in schemes(levels - 1).values():
        need = Reduction.landing([1] + [len(stage) for stage in kind], D)
        land, sems = max(land, need[0]), max(sems, need[1])
    scratch = [
        vm(T, D, bf), vm(T, D, bf), vm(D, 3 * D, bf), vm(D, D, bf), vm(D, FF, bf), vm(FF, D, bf),
        vm(T, D, bf), vm(T + FRONT + 16, 2 * D, bf), vm(NG * 16, 2 * D, bf),
        vm(D, T, bf), vm(256, D, bf), vm(D, T, bf), vm(NG * KEYS, D, bf),
        vm(T, D, f32), vm(T, D, bf), vm(D, T, bf), vm(D, T, bf),
        vm(T + FRONT + 16, D, f32), vm(T, D, f32), vm(T, FFC, bf), vm(T, FFC, bf),
        vm(NG * 16, 256, bf), vm(KEYS, 128, f32), vm(NG, 8, 128, f32),
        vm(NG, 8, 128, f32), vm(80, D, bf),
        vm(2, 48, D, bf), vm(2, 16, D, bf), vm(2, 48, D, bf), vm(2, 16, D, bf),
        vm(nu, D, D, bf), vm(nu, land, D, bf), vm(2, land, 768, bf),
        vm(8, D, f32), vm(levels, 8, D, f32), vm(NS, D, bf), vm(NS, 2 * D, bf),
        dma(6), dma(5), dma(6), dma(6),
        dma(nu + 2, sems), dma(nu + 2, sems), dma(levels), dma(levels),
        pltpu.SemaphoreType.REGULAR((nu + 2, levels)),
    ]
    row = lambda v: v.reshape(1, D)
    out, gframes, units, uqkv, small = pl.pallas_call(
        functools.partial(body, ntm, (T, D, FF, NU)),
        out_shape=[
            jax.ShapeDtypeStruct((T, D), bf),
            jax.ShapeDtypeStruct((T, D), f32),
            jax.ShapeDtypeStruct((nu, D, D), bf),
            jax.ShapeDtypeStruct((D, 3 * D), bf),
            jax.ShapeDtypeStruct((8, D), f32),
        ],
        in_specs=[A] * 6 + [V] * 5,
        out_specs=[A] * 5,
        scratch_shapes=scratch,
        compiler_params=pltpu.CompilerParams(
            vmem_limit_bytes=63 * 2**20, collective_id=0, has_side_effects=True
        ),
    )(frames[0], dy[0], wqkv, wo, wu, wd, lens, row(ga), row(ba), row(gf), row(bfn))
    parts = FFC // 256
    steps = NC * parts
    part, tile = D // steps, T // steps
    spec = lambda shape, index: pl.BlockSpec(shape, index)
    down, up, gout, gqkv, out, gframes, *vectors = pl.pallas_call(
        finish,
        grid=(steps,),
        out_shape=[
            jax.ShapeDtypeStruct((FF, D), f32),
            jax.ShapeDtypeStruct((D, FF), f32),
            jax.ShapeDtypeStruct((D, D), f32),
            jax.ShapeDtypeStruct((D, 3 * D), f32),
            jax.ShapeDtypeStruct((T, D), bf),
            jax.ShapeDtypeStruct((T, D), f32),
        ]
        + [jax.ShapeDtypeStruct((1, D), f32)] * 4,
        in_specs=[
            spec((1, D, 256), lambda k: (k // parts, 0, k % parts)),
            spec((1, D, 256), lambda k: (NC + k // parts, 0, k % parts)),
            spec((1, part, D), lambda k: (2 * NC, k, 0)),
            spec((part, 3 * D), lambda k: (k, 0)),
            spec((tile, D), lambda k: (k, 0)),
            spec((tile, D), lambda k: (k, 0)),
            spec((8, D), lambda k: (0, 0)),
        ],
        out_specs=[
            spec((256, D), lambda k: (k, 0)),
            spec((D, 256), lambda k: (0, k)),
            spec((part, D), lambda k: (k, 0)),
            spec((part, 3 * D), lambda k: (k, 0)),
            spec((tile, D), lambda k: (k, 0)),
            spec((tile, D), lambda k: (k, 0)),
        ]
        + [spec((1, D), lambda k: (0, 0))] * 4,
        compiler_params=pltpu.CompilerParams(vmem_limit_bytes=62 * 2**20),
    )(units, units, units, uqkv, out, gframes, small)
    return (
        out[None], gframes[None], gqkv, gout, up, down,
        *[v.reshape(D) for v in vectors],
    )


def solution(mesh):
    big, rep = P("rows", "tm", None), P()
    return jax.shard_map(
        local,
        mesh=mesh,
        in_specs=(big, P("rows", None)) + (rep,) * 8 + (big,),
        out_specs=(big, big) + (rep,) * 8,
        check_vma=False,
    )
```

time: 332 us -> 160 us (0.48)
  waiting for transfers between devices: 114 us -> 0 us
  blocking collectives: 38.5 us -> 0 us
  local copies, waits for them, and re-layouts: 33.8 us -> 0 us
  Pallas kernels: 127 us -> 159 us
  between operations: 14.1 us -> 0.83 us
  other arithmetic: 4.51 us -> 0 us
    psum x1 -> x0, waiting for transfers between devices: 114 us -> none  [local(): units = lax.psum(units, ('tm', 'rows')).astype(f32)]
    psum x1 -> x0, blocking collectives: 38.5 us -> none  [local(): small = lax.psum(small, ('tm', 'rows'))]
    pallas_call x1, Pallas kernels: 127 us -> 147 us  [local(): pl.pallas_call(functools.partial(body, ntm, (T, D, FF, NU)), out_shape=[j...]
    transpose x5 -> x0, local copies, waits for them, and re-layouts: 17.5 us -> none  [the longest x2 9.59 us: local(): units[:n].transpose(0, 2, 1).reshape(FF, D)]
    unnamed x10 -> x0, local copies, waits for them, and re-layouts: 14.7 us -> none
    pallas_call x0 -> x1, Pallas kernels: none -> 12.4 us  [local(): pl.pallas_call(finish, grid=(steps,), out_shape=[jax.ShapeDtypeStruct((FF...]
    convert_element_type x1 -> x0, other arithmetic: 4.51 us -> none  [local(): units = lax.psum(units, ('tm', 'rows')).astype(f32)]
  transfers between devices with their start and end apart: 1 -> 0, of which waited for: 1 -> 0; matrix products, arithmetic and copies ran while one was open for 0% -> 0% of each run, Pallas kernels for 0% -> 0%
where the time goes in v2:
time: 160 us
  Pallas kernels  159 us (99%)
    pallas_call x1, Pallas kernels, local(): pl.pallas_call(functools.partial(body, ntm, (T, D, FF, NU)), out_shape=[j...  147 us
    pallas_call x1, Pallas kernels, local(): pl.pallas_call(finish, grid=(steps,), out_shape=[jax.ShapeDtypeStruct((FF...  12.4 us

profile of v2, /device:TPU:0, one launch (start us, length us, event | category | flops | bytes accessed | tf_op | source)
XLA Modules:
  0.0 160.0 jit_solution(15716624211383799005)
XLA Ops:
  0.6 146.8 %shard_map.186 = (bf16[2048,512]{1,0:T(8,128)(2,1)}, f32[2048,512]{1,0:T(8,128)}, bf16[9,512,512]{2,1,0:T(8,128)(2,1)}, bf16[512,1536]{1,0:T(8,128)(2,1)}, f32[8,512]{1,0:T(8,128)}) custom-call(bf16[2048,512]{1,0:T(8,128)(2,1)} %bitcast.12, bf16[2048,512]{1,0:T(8,128)(2,1)} %bitcast.13, bf16[512,1536]{1,0:T(8,128)(2,1)} %refs_2_.1, ...), custom_call_target="tpu_custom_call" | custom-call | tf_op jit(solution)/shard_map/pallas_call | solution.py:636
  147.4 12.4 %shard_map.187 = (f32[2048,512]{1,0:T(8,128)}, f32[512,2048]{1,0:T(8,128)}, f32[512,512]{1,0:T(8,128)}, f32[512,1536]{1,0:T(8,128)}, bf16[2048,512]{1,0:T(8,128)...) custom-call(bf16[9,512,512]{2,1,0:T(8,128)(2,1)} %get-tuple-element., ...), custom_call_target="tpu_custom_call" | custom-call | tf_op jit(solution)/shard_map/pallas_call | solution.py:656

commit v3 on v2

--- a/solution.py
+++ b/solution.py
@@ -20,10 +20,11 @@
 bf = jnp.bfloat16
 f32 = jnp.float32
 MESH = pl.DeviceIdType.MESH
-ORDER = "10031110qqq"
+ORDER = ["01"] * 9 + ["q", "q"]
 GAPS = {
-    "0": [1, 5, 4, 3, 3, 3, 3, 4, 5, 1],
-    "q": [1, 5, 4, 4, 5, 1],
+    "0": [1, 4, 3, 3, 4, 3, 3, 4, 1],
+    "p": [1, 5, 3, 3, 3, 5, 1],
+    "q": [1, 4, 3, 3, 4, 1],
 }
 
 
@@ -82,9 +83,9 @@
         self.pos, self.rest = 0, 0
         self.levels = []
         lo, size, at, sem = 0, rows, 0, 0
-        for axes in stages:
+        for n, axes in enumerate(stages):
             k = len(axes)
-            split = size % (16 << k) == 0
+            split = size % (16 << k) == 0 and (k > 1 or n < len(stages) - 1)
             part = size >> k if split else size
             rank = sum(bit * 2**j for j, (bit, _) in enumerate(axes))
             peers = []
@@ -109,8 +110,9 @@
     @staticmethod
     def landing(stages, rows):
         size, at, sem = rows, 0, 0
-        for k in stages:
-            size = size >> k if size % (16 << k) == 0 else size
+        for n, k in enumerate(stages):
+            split = size % (16 << k) == 0 and (k > 1 or n < len(stages) - 1)
+            size = size >> k if split else size
             at += size * ((1 << k) - 1)
             sem += 2 * ((1 << k) - 1)
         return at, sem
@@ -173,6 +175,7 @@
         "1": one(low[::-1] + high),
         "2": one(high + low),
         "3": one(high + low[::-1]),
+        "p": [low] + one(high),
         "q": [low] + [high[i : i + 2] for i in range(0, len(high), 2)],
     }
 
@@ -185,11 +188,11 @@
     nu = 2 * NC + 1
     (
         frames_h, dy_h, wqkv_h, wo_h, wu_h, wd_h, lens, ga, ba, gf, bfn,
-        out_h, gframes_h, units_h, uqkv_h, small_h,
+        out_h, gframes_h, units_h, uqkv_h, small_h, acts_h, mid_h,
         X, DY, wqkv, wo, wu, wd,
         Q, KV, MW, NT_, SUMM, ATTT, PR, MID, N2, N2T, DYT, OUT, D2, ACT, DH,
-        SEL, KR, LO, HI, HX, HRL, HRR, SNL, SNR, U, UR, UQR, SMALL, SMR, DSUM, DMK,
-        lsem, osem, ssem, rsem, ussem, ursem, xssem, xrsem, freed,
+        SEL, KR, LOHI, HX, HRL, HRR, SNL, SNR, U, UR, UQR, SMALL, SMR,
+        lsem, osem, ssem, rsem, ussem, ursem, xssem, xrsem, freed, asem, bsem,
     ) = refs
     me, row_id = lax.axis_index("tm"), lax.axis_index("rows")
     right = lax.rem(me + 1, ntm)
@@ -201,7 +204,7 @@
             [(frames_h, X), (wqkv_h, wqkv), (dy_h, DY), (wo_h, wo), (wu_h, wu), (wd_h, wd)]
         )
     ]
-    for load in loads:
+    for load in loads[:2]:
         load.start()
 
     bits = ntm.bit_length() - 1
@@ -251,15 +254,24 @@
                 def _():
                     slot()
 
+    def reduce_block(k, kind, own, got, width):
+        for part, order in enumerate(kind):
+            cols = pl.ds(part * (width // len(kind)), width // len(kind))
+            reduction(
+                2 * k + part, order, D,
+                lambda lo, n, cols=cols: own(rows_of(lo, n), cols),
+                lambda lo, n, cols=cols: got(pl.ds(lo, n), cols),
+            )
+
     def reduce_unit(k, kind):
-        reduction(
-            k, kind, D,
-            lambda lo, n: U.at[k, rows_of(lo, n)],
-            lambda lo, n: UR.at[k, lo : lo + n],
+        reduce_block(
+            k, kind, lambda r, c: U.at[k, r, c], lambda r, c: UR.at[k, r, c], D
         )
 
-    for load in loads[:3]:
+    for load in loads[:2]:
         load.wait()
+    for load in loads[2:]:
+        load.start()
     gain1, bias1 = ga[...], ba[...]
     NM = TT // SEG
     mean16 = jnp.where(
@@ -274,7 +286,6 @@
         SUMM[rows_of(i * NM, NM), :] = nn(mean16, nb).astype(bf)
         Q[r, :] = (nn(nb, wqkv[:, :D]) * HEAD_DIM**-0.5).astype(bf)
         KV[rows_of(i * TT + FRONT, TT), :] = nn(nb, wqkv[:, D:]).astype(bf)
-        DYT[:, rows_of(i * TT, TT, 128)] = DY[r, :].T
         return 0
 
     lax.fori_loop(0, T // TT, project, 0)
@@ -313,28 +324,30 @@
         st, en = MID[0:NU, 0:128], MID[0:NU, 128:256]
         lo = jnp.max(jnp.where(st <= seg, st, -1.0), axis=0, keepdims=True) - base
         hi = jnp.min(jnp.where(en > seg, en, 1e9), axis=0, keepdims=True) - base
-        LO[g] = jnp.broadcast_to(lo, (8, 128))
-        HI[g] = jnp.broadcast_to(hi, (8, 128))
+        LOHI[g] = jnp.where(iota((8, 128), 0) == 0, lo, hi)
         return 0
 
     lax.fori_loop(0, NG, bounds, 0)
-    r512, c256 = iota((NG * 16, 256), 0), iota((NG * 16, 256), 1)
-    seg = 4 * jnp.right_shift(r512, 4) - 4 + (r512 & 15)
-    src = jnp.where(seg < 0, seg + 4 + NS, seg)
-    SEL[...] = jnp.where(((r512 & 15) < 8) & (src == c256), 1.0, 0.0).astype(bf)
+    rows, cols = iota((NG * 16, NS), 0), iota((NG * 16, NS), 1)
+    seg = 4 * jnp.right_shift(rows, 4) - 4 + (rows & 15)
+    SEL[...] = jnp.where(((rows & 15) < 8) & (seg == cols), 1.0, 0.0).astype(bf)
     SMALL[...] = jnp.zeros_like(SMALL)
 
-    to_right.wait()
-    to_left.wait()
-    xhat, _r = standardise(HX[...].astype(f32))
-    nb = (xhat * gain1 + bias1).astype(bf)
-    edge = nn(nb, wqkv[:, D:]).astype(bf)
-    KV[0:FRONT, :] = edge[32:64]
-    KV[T + FRONT : T + FRONT + 16, :] = edge[64:80]
-    SUMM[NS:256, :] = jnp.zeros((256 - NS, D), bf)
-    SUMM[NS : NS + 16, :] = nn(mean16[:16, :64], nb[:64]).astype(bf)
     MW[...] = nn(SEL[...], nn(SUMM[...], wqkv[:, D:]).astype(bf)).astype(bf)
 
+    def edges():
+        to_right.wait()
+        to_left.wait()
+        xhat, _r = standardise(HX[...].astype(f32))
+        nb = (xhat * gain1 + bias1).astype(bf)
+        edge = nn(nb, wqkv[:, D:]).astype(bf)
+        KV[0:FRONT, :] = edge[32:64]
+        KV[T + FRONT : T + FRONT + 16, :] = edge[64:80]
+        mem = nn(nn(mean16[:16, :64], nb[:64]).astype(bf), wqkv[:, D:])
+        now = MW[0:16, :].astype(f32)
+        MW[0:16, :] = jnp.where(iota((16, 1), 0) < 4, mem, now).astype(bf)
+
+    loads[2].wait()
     loads[3].wait()
     gain2, bias2 = gf[...], bfn[...]
 
@@ -343,7 +356,12 @@
         mem = rows_of(g * MEMROWS, MEMROWS)
         return jnp.concatenate([MW[mem, c], KV[win, c]], axis=0)
 
-    def attend(i, _):
+    def attend(step, _):
+        @pl.when(step == T // TT - 2)
+        def _():
+            edges()
+
+        i = lax.rem(step + 1, T // TT)
         r = rows_of(i * TT, TT)
         gs = [i * GI + j for j in range(GI)]
         for j, g in enumerate(gs):
@@ -352,7 +370,7 @@
                 q4 = spread_heads(Q[rows_of(g * GROUP, GROUP), c])
                 OUT[KEYS * j : KEYS * j + KEYS, c] = nt(window(g, c), q4)
         for j, g in enumerate(gs):
-            lo, hi = LO[g][0:1], HI[g][0:1]
+            lo, hi = LOHI[g, 0:1, :], LOHI[g, 1:2, :]
             kr = KR[...]
             ok = (kr >= lo) & (kr < hi)
             for p in range(D // 128):
@@ -371,6 +389,7 @@
             tiles.append(jnp.concatenate(cols, axis=1))
         att = jnp.concatenate(tiles, axis=0).astype(bf)
         ATTT[:, rows_of(i * TT, TT, 128)] = att.T
+        DYT[:, rows_of(i * TT, TT, 128)] = DY[r, :].T
         mid = X[r, :].astype(f32) + nn(att, wo[...])
         MID[r, :] = mid
         xhat, _r = standardise(mid)
@@ -383,6 +402,12 @@
 
     loads[4].wait()
     loads[5].wait()
+    keep_mid = pltpu.make_async_copy(MID, mid_h, bsem.at[NC])
+    keep_mid.start()
+
+    def keep_act(c, i, r):
+        return pltpu.make_async_copy(ACT.at[r], acts_h.at[c, r], asem.at[i])
+
     for c in range(NC):
         cs = slice(c * FFC, (c + 1) * FFC)
 
@@ -394,21 +419,17 @@
             da = nt(DY[r, :], wd[cs, :])
             phi = 0.5 + 0.5 * lax.erf(h * 0.7071067811865476)
             slope = phi + h * (jnp.exp(h * h * -0.5) * 0.3989422804014327)
-            a = (h * phi).astype(bf)
             d = (da * slope).astype(bf)
-            ACT[r, :] = a
+            if c:
+                keep_act(c - 1, i, r).wait()
+            ACT[r, :] = (h * phi).astype(bf)
+            keep_act(c, i, r).start()
             DH[r, :] = d
-            o = nn(a, wd[cs, :])
             d2 = nt(d, wu[:, cs])
-            if c == 0:
-                OUT[r, :] = MID[r, :] + o
-                D2[r, :] = d2
-            elif c < NC - 1:
-                OUT[r, :] += o
+            if c:
                 D2[r, :] += d2
             else:
-                N2[r, :] = (OUT[r, :] + o).astype(bf)
-                D2[r, :] += d2
+                D2[r, :] = d2
             return 0
 
         lax.fori_loop(0, T // TT, ffn, 0)
@@ -418,9 +439,6 @@
         U[NC + c] = nn(N2T[...], DH[...]).astype(bf)
         reduce_unit(NC + c, ORDER[2 * c + 1])
         slot()
-
-    store_out = pltpu.make_async_copy(N2, out_h, osem.at[0])
-    store_out.start()
 
     def back_mid(i, _):
         slots(i, T // TT)
@@ -433,6 +451,7 @@
         dmid = DY[r, :].astype(f32) + norm_grad(d2, xhat, rstd, gain2)
         D2[r, :] = dmid
         db = dmid.astype(bf)
+        keep_act(NC - 1, i, r).wait()
         ACT[r, :] = db
         DH[r, :] = nt(db, wo[...]).astype(bf)
         return 0
@@ -440,6 +459,14 @@
     lax.fori_loop(0, T // TT, back_mid, 0)
     U[2 * NC] = nn(ATTT[...], ACT[...]).astype(bf)
     reduce_unit(2 * NC, ORDER[2 * NC])
+
+    homes = [DY.at[0:T], PR.at[0:T], PR.at[T : 2 * T], DH.at[0:T]]
+    fetches = [
+        pltpu.make_async_copy(acts_h.at[c], homes[c], bsem.at[c]) for c in range(NC)
+    ]
+    fetches.append(pltpu.make_async_copy(mid_h, MID, bsem.at[NC]))
+    fetches[0].start()
+    keep_mid.wait()
 
     for h in range(2):
         c = slice(256 * h, 256 * h + 256)
@@ -500,6 +527,11 @@
             return 0
 
         lax.fori_loop(0, NG // GI, back_att, 0)
+        if h:
+            for fetch in fetches[1:]:
+                fetch.start()
+        at = 768 * h
+        N2T[:, at : at + 256] = nn(NT_[...], Q[:, c]).astype(bf)
         give_left.wait()
         give_right.wait()
         live_l = jnp.where(me < ntm - 1, 1.0, 0.0).astype(f32)
@@ -511,7 +543,7 @@
         ).astype(bf)
         dmw = jnp.concatenate([MW[:, c], MW[:, cv]], axis=1)
         dmk = tn(SEL[:, 0:NS], dmw) + nn(pick, HRL[h, FRONT : FRONT + 16, :]) * live_l
-        DMK[:, 512 * h : 512 * h + 512] = dmk.astype(bf)
+        N2[NS * h : NS * h + NS, :] = dmk.astype(bf)
 
         def to_low(i, _, c=c, cv=cv):
             r = rows_of(i * TT + FRONT, TT)
@@ -521,18 +553,17 @@
 
         lax.fori_loop(0, T // TT, to_low, 0)
         own = slice(FRONT, T + FRONT)
-        at = 768 * h
-        N2T[:, at : at + 256] = nn(NT_[...], Q[:, c]).astype(bf)
         N2T[:, at + 256 : at + 512] = (
-            nn(NT_[...], KV[own, c]) + tn(SUMM[0:NS, :], DMK[:, 512 * h : 512 * h + 256])
+            nn(NT_[...], KV[own, c]) + tn(SUMM[0:NS, :], N2[NS * h : NS * h + NS, 0:256])
         ).astype(bf)
         N2T[:, at + 512 : at + 768] = (
-            nn(NT_[...], KV[own, cv]) + tn(SUMM[0:NS, :], DMK[:, 512 * h + 256 : 512 * h + 512])
+            nn(NT_[...], KV[own, cv]) + tn(SUMM[0:NS, :], N2[NS * h : NS * h + NS, 256:512])
         ).astype(bf)
-        reduction(
-            nu + h, ORDER[2 * NC + 1 + h], D,
-            lambda lo, n, at=at: N2T.at[rows_of(lo, n), at : at + 768],
-            lambda lo, n, h=h: UQR.at[h, lo : lo + n],
+        reduce_block(
+            nu + h, ORDER[2 * NC + 1 + h],
+            lambda r, c, at=at: N2T.at[r, pl.ds(at + c.start, c.size)],
+            lambda r, c, h=h: UQR.at[h, r, c],
+            768,
         )
         slot()
 
@@ -540,8 +571,8 @@
     for h in range(2):
         for k in range(2):
             lo = D * (1 + k) + 256 * h
-            dsum += nt(DMK[:, 512 * h + 256 * k : 512 * h + 256 * k + 256], wqkv[:, lo : lo + 256])
-    DSUM[...] = (dsum * (1.0 / SEG)).astype(bf)
+            dsum += nt(N2[NS * h : NS * h + NS, 256 * k : 256 * k + 256], wqkv[:, lo : lo + 256])
+    N2[2 * NS : 3 * NS, :] = (dsum * (1.0 / SEG)).astype(bf)
     widen = jnp.where(
         jnp.right_shift(iota((TT, NM), 0), 4) == iota((TT, NM), 1), 1.0, 0.0
     ).astype(bf)
@@ -552,36 +583,93 @@
         r = rows_of(i * TT, TT)
         rk = rows_of(i * TT + FRONT, TT)
         dn = nt(Q[r, :], wqkv[:, :D]) + nt(KV[rk, :], wqkv[:, D:])
-        dn = dn + nn(widen, DSUM[rows_of(i * NM, NM), :])
+        dn = dn + nn(widen, N2[rows_of(i * NM + 2 * NS, NM), :])
         xhat, rstd = standardise(X[r, :].astype(f32))
         SMALL[0:1, :] += jnp.sum(dn * xhat, axis=0, keepdims=True)
         SMALL[1:2, :] += jnp.sum(dn, axis=0, keepdims=True)
         D2[r, :] += norm_grad(dn, xhat, rstd, gain1)
+        give_back(i, r).start()
         return 0
 
+    def give_back(i, r):
+        return pltpu.make_async_copy(D2.at[r], gframes_h.at[r], asem.at[i])
+
     lax.fori_loop(0, T // TT, back_in, 0)
-    store_g = pltpu.make_async_copy(D2, gframes_h, osem.at[1])
-    store_g.start()
-
-    def small_copy(k):
-        return pltpu.make_async_remote_copy(
-            src_ref=SMALL, dst_ref=SMR.at[k], send_sem=xssem.at[k], recv_sem=xrsem.at[k],
-            device_id=flipped([axes[k]]), device_id_type=MESH,
-        )
-
-    for k in range(bits + 1):
-        small_copy(k).start()
-        slot(True)
-        small_copy(k).wait()
-        SMALL[...] += SMR[k]
+
+    small_stages, base, sem = [], 0, 0
+    for stage in [[0]] + [[1 + b for b in stage] for stage in kinds["q"]]:
+        some = [axes[a] for a in stage]
+        rank = sum(bit * 2**j for j, (bit, _) in enumerate(some))
+        peers = [
+            flipped([a for j, a in enumerate(some) if (m >> j) & 1]) for m in range(1, 1 << len(some))
+        ]
+        small_stages.append((base + rank, base, 1 << len(some), peers, sem))
+        base, sem = base + (1 << len(some)), sem + len(peers)
+
+    def small_copies(k):
+        mine, _, _, peers, sem = small_stages[k]
+        return [
+            pltpu.make_async_remote_copy(
+                src_ref=SMR.at[mine], dst_ref=SMR.at[mine], send_sem=xssem.at[sem + q],
+                recv_sem=xrsem.at[sem + q], device_id=peer, device_id_type=MESH,
+            )
+            for q, peer in enumerate(peers)
+        ]
+
+    def small_step(k):
+        if 0 < k <= len(small_stages):
+            for copy in small_copies(k - 1):
+                copy.wait()
+            _, base, count, _, _ = small_stages[k - 1]
+            total = SMR[base]
+            for q in range(1, count):
+                total = total + SMR[base + q]
+            SMALL[...] = total
+        if k < len(small_stages):
+            SMR[small_stages[k][0]] = SMALL[...]
+            for copy in small_copies(k):
+                copy.start()
+
+    small_step(0)
+
+    for fetch in fetches:
+        fetch.wait()
+
+    def put_out(i, r):
+        return pltpu.make_async_copy(N2.at[r], out_h.at[r], bsem.at[i])
+
+    def down(i, _):
+        slots(i, T // TT)
+        for k in range(1, T // TT):
+
+            @pl.when(i == k)
+            def _(k=k):
+                small_step(k)
+
+        r = rows_of(i * TT, TT)
+        total = MID[r, :]
+        for c, home in enumerate(homes):
+            total = total + nn(home[r, :], wd[c * FFC : (c + 1) * FFC, :])
+        N2[r, :] = total.astype(bf)
+        put_out(i, r).start()
+        return 0
+
+    lax.fori_loop(0, T // TT, down, 0)
+    for k in range(T // TT, len(small_stages) + 1):
+        small_step(k)
+    store_s = pltpu.make_async_copy(SMALL, small_h, osem.at[4])
+    store_s.start()
     while active:
         slot(True)
     store_u = pltpu.make_async_copy(U, units_h, osem.at[2])
     store_q = pltpu.make_async_copy(N2T.at[:, 0 : 3 * D], uqkv_h, osem.at[3])
-    store_s = pltpu.make_async_copy(SMALL, small_h, osem.at[4])
+    store_u.start()
+    store_q.start()
+    for i in range(T // TT):
+        r = pl.ds(i * TT, TT)
+        give_back(i, r).wait()
+        put_out(i, r).wait()
     for store in (store_u, store_q, store_s):
-        store.start()
-    for store in (store_out, store_g, store_u, store_q, store_s):
         store.wait()
 
 
@@ -620,20 +708,20 @@
     scratch = [
         vm(T, D, bf), vm(T, D, bf), vm(D, 3 * D, bf), vm(D, D, bf), vm(D, FF, bf), vm(FF, D, bf),
         vm(T, D, bf), vm(T + FRONT + 16, 2 * D, bf), vm(NG * 16, 2 * D, bf),
-        vm(D, T, bf), vm(256, D, bf), vm(D, T, bf), vm(NG * KEYS, D, bf),
+        vm(D, T, bf), vm(NS, D, bf), vm(D, T, bf), vm(NG * KEYS, D, bf),
         vm(T, D, f32), vm(T, D, bf), vm(D, T, bf), vm(D, T, bf),
         vm(T + FRONT + 16, D, f32), vm(T, D, f32), vm(T, FFC, bf), vm(T, FFC, bf),
-        vm(NG * 16, 256, bf), vm(KEYS, 128, f32), vm(NG, 8, 128, f32),
-        vm(NG, 8, 128, f32), vm(80, D, bf),
+        vm(NG * 16, NS, bf), vm(KEYS, 128, f32), vm(NG, 8, 128, f32),
+        vm(80, D, bf),
         vm(2, 48, D, bf), vm(2, 16, D, bf), vm(2, 48, D, bf), vm(2, 16, D, bf),
         vm(nu, D, D, bf), vm(nu, land, D, bf), vm(2, land, 768, bf),
-        vm(8, D, f32), vm(levels, 8, D, f32), vm(NS, D, bf), vm(NS, 2 * D, bf),
+        vm(8, D, f32), vm(2 * levels, 8, D, f32),
         dma(6), dma(5), dma(6), dma(6),
-        dma(nu + 2, sems), dma(nu + 2, sems), dma(levels), dma(levels),
-        pltpu.SemaphoreType.REGULAR((nu + 2, levels)),
+        dma(2 * nu + 4, sems), dma(2 * nu + 4, sems), dma(2 * levels), dma(2 * levels),
+        pltpu.SemaphoreType.REGULAR((2 * nu + 4, levels)), dma(T // TT), dma(max(NC + 1, T // TT)),
     ]
     row = lambda v: v.reshape(1, D)
-    out, gframes, units, uqkv, small = pl.pallas_call(
+    out, gframes, units, uqkv, small, _, _ = pl.pallas_call(
         functools.partial(body, ntm, (T, D, FF, NU)),
         out_shape=[
             jax.ShapeDtypeStruct((T, D), bf),
@@ -641,15 +729,17 @@
             jax.ShapeDtypeStruct((nu, D, D), bf),
             jax.ShapeDtypeStruct((D, 3 * D), bf),
             jax.ShapeDtypeStruct((8, D), f32),
+            jax.ShapeDtypeStruct((NC, T, FFC), bf),
+            jax.ShapeDtypeStruct((T, D), f32),
         ],
         in_specs=[A] * 6 + [V] * 5,
-        out_specs=[A] * 5,
+        out_specs=[A] * 7,
         scratch_shapes=scratch,
         compiler_params=pltpu.CompilerParams(
-            vmem_limit_bytes=63 * 2**20, collective_id=0, has_side_effects=True
+            vmem_limit_bytes=64 * 2**20 - 2**18, collective_id=0, has_side_effects=True
         ),
     )(frames[0], dy[0], wqkv, wo, wu, wd, lens, row(ga), row(ba), row(gf), row(bfn))
-    parts = FFC // 256
+    parts = FFC // 512
     steps = NC * parts
     part, tile = D // steps, T // steps
     spec = lambda shape, index: pl.BlockSpec(shape, index)
@@ -666,8 +756,8 @@
         ]
         + [jax.ShapeDtypeStruct((1, D), f32)] * 4,
         in_specs=[
-            spec((1, D, 256), lambda k: (k // parts, 0, k % parts)),
-            spec((1, D, 256), lambda k: (NC + k // parts, 0, k % parts)),
+            spec((1, D, 512), lambda k: (k // parts, 0, k % parts)),
+            spec((1, D, 512), lambda k: (NC + k // parts, 0, k % parts)),
             spec((1, part, D), lambda k: (2 * NC, k, 0)),
             spec((part, 3 * D), lambda k: (k, 0)),
             spec((tile, D), lambda k: (k, 0)),
@@ -675,8 +765,8 @@
             spec((8, D), lambda k: (0, 0)),
         ],
         out_specs=[
-            spec((256, D), lambda k: (k, 0)),
-            spec((D, 256), lambda k: (0, k)),
+            spec((512, D), lambda k: (k, 0)),
+            spec((D, 512), lambda k: (0, k)),
             spec((part, D), lambda k: (k, 0)),
             spec((part, 3 * D), lambda k: (k, 0)),
             spec((tile, D), lambda k: (k, 0)),

time: 160 us -> 146 us (0.912)
  Pallas kernels: 159 us -> 145 us
    pallas_call x1, Pallas kernels: 147 us -> 133 us  [local(): pl.pallas_call(functools.partial(body, ntm, (T, D, FF, NU)), out_shape=[j...]
where the time goes in v3:
time: 146 us
  Pallas kernels  145 us (99%)
    pallas_call x1, Pallas kernels, local(): pl.pallas_call(functools.partial(body, ntm, (T, D, FF, NU)), out_shape=[j...  133 us
    pallas_call x1, Pallas kernels, local(): pl.pallas_call(finish, grid=(steps,), out_shape=[jax.ShapeDtypeStruct((FF...  12 us

profile of v3, /device:TPU:0, one launch (start us, length us, event | category | flops | bytes accessed | tf_op | source)
XLA Modules:
  0.0 146.0 jit_solution(17386284539133166835)
XLA Ops:
  0.6 133.2 %shard_map.186 = (bf16[2048,512]{1,0:T(8,128)(2,1)}, f32[2048,512]{1,0:T(8,128)}, bf16[9,512,512]{2,1,0:T(8,128)(2,1)}, bf16[512,1536]{1,0:T(8,128)(2,1)}, f32[8...) custom-call(bf16[2048,512]{1,0:T(8,128)(2,1)} %bitcast.12, bf16[2048,512]{1,0:T(8,128)(2,1)} %bitcast.13, ...), custom_call_target="tpu_custom_call" | custom-call | tf_op jit(solution)/shard_map/pallas_call | solution.py:724
  133.8 12.0 %shard_map.187 = (f32[2048,512]{1,0:T(8,128)}, f32[512,2048]{1,0:T(8,128)}, f32[512,512]{1,0:T(8,128)}, f32[512,1536]{1,0:T(8,128)}, bf16[2048,512]{1,0:T(8,128)...) custom-call(bf16[9,512,512]{2,1,0:T(8,128)(2,1)} %get-tuple-element., ...), custom_call_target="tpu_custom_call" | custom-call | tf_op jit(solution)/shard_map/pallas_call | solution.py:746

commit v4 on v3

--- a/solution.py
+++ b/solution.py
@@ -20,7 +20,9 @@
 bf = jnp.bfloat16
 f32 = jnp.float32
 MESH = pl.DeviceIdType.MESH
-ORDER = ["01"] * 9 + ["q", "q"]
+ORDER = ["01"] * 9 + ["qqq", "qqq"]
+ENDS = [[2], [2]]
+SPREAD = [1.5, 1.4, 1.2, 1.0, 1.5, 1.4, 1.2, 1.0, 1.0, 1.0, 1.0]
 GAPS = {
     "0": [1, 4, 3, 3, 4, 3, 3, 4, 1],
     "p": [1, 5, 3, 3, 3, 5, 1],
@@ -76,11 +78,11 @@
 
 
 class Reduction:
-    def __init__(self, stages, rows, own, got, sems, gaps, name):
-        self.own, self.got, self.name = own, got, name
+    def __init__(self, stages, rows, own, got, sems, gaps, store):
+        self.own, self.got, self.store = own, got, store
         self.ssem, self.rsem, self.freed = sems
         self.gaps = gaps
-        self.pos, self.rest = 0, 0
+        self.pos, self.rest = 0, 0.0
         self.levels = []
         lo, size, at, sem = 0, rows, 0, 0
         for n, axes in enumerate(stages):
@@ -162,7 +164,7 @@
                 pl.semaphore_wait(self.freed.at[i], len(self.levels[i][0]))
             for copy in self.copies(self.pos):
                 copy.start()
-            self.rest = self.gaps[min(self.pos, len(self.gaps) - 1)]
+            self.rest += self.gaps[min(self.pos, len(self.gaps) - 1)]
         self.pos += 1
         return self.pos > len(self.steps)
 
@@ -233,18 +235,20 @@
         )
 
     kinds = schemes(bits)
-    active = []
-
-    def reduction(k, kind, rows, own, got):
+    active, stored = [], []
+
+    def reduction(k, kind, rows, own, got, store, spread):
         stages = [[axes[0]]] + [[axes[1 + b] for b in stage] for stage in kinds[kind]]
-        gaps = GAPS[kind] if kind in GAPS else GAPS["0"]
-        active.append(Reduction(stages, rows, own, got, (ussem.at[k], ursem.at[k], freed.at[k]), gaps, k))
+        gaps = [spread * gap for gap in GAPS.get(kind, GAPS["0"])]
+        active.append(Reduction(stages, rows, own, got, (ussem.at[k], ursem.at[k], freed.at[k]), gaps, store))
 
     def slot(every=False):
         for red in list(active):
             red.rest -= 1
-            if (red.rest <= 0 or every) and red.advance():
+            if (red.rest <= 0.01 or every) and red.advance():
                 active.remove(red)
+                red.store.start()
+                stored.append(red.store)
 
     def slots(i, count):
         for k in range(count):
@@ -254,18 +258,32 @@
                 def _():
                     slot()
 
-    def reduce_block(k, kind, own, got, width):
+    def reduce_unit(k, kind):
         for part, order in enumerate(kind):
-            cols = pl.ds(part * (width // len(kind)), width // len(kind))
+            cols = pl.ds(part * (D // len(kind)), D // len(kind))
             reduction(
                 2 * k + part, order, D,
-                lambda lo, n, cols=cols: own(rows_of(lo, n), cols),
-                lambda lo, n, cols=cols: got(pl.ds(lo, n), cols),
+                lambda lo, n, cols=cols: U.at[k, rows_of(lo, n), cols],
+                lambda lo, n, cols=cols: UR.at[k, pl.ds(lo, n), cols],
+                pltpu.make_async_copy(
+                    U.at[k, :, cols], units_h.at[k, :, cols], osem.at[2 * k + part]
+                ),
+                SPREAD[k],
             )
 
-    def reduce_unit(k, kind):
-        reduce_block(
-            k, kind, lambda r, c: U.at[k, r, c], lambda r, c: UR.at[k, r, c], D
+    def reduce_part(h, p):
+        if p not in ENDS[h]:
+            return
+        first = max([e + 1 for e in ENDS[h] if e < p], default=0)
+        k, at, n256 = 2 * nu + 3 * h + p, 768 * h + 256 * first, 256 * (p + 1 - first)
+        reduction(
+            k, ORDER[2 * NC + 1 + h][p], D,
+            lambda lo, n: N2T.at[rows_of(lo, n), at : at + n256],
+            lambda lo, n: UQR.at[h, lo : lo + n, 256 * first : 256 * first + n256],
+            pltpu.make_async_copy(
+                N2T.at[:, at : at + n256], uqkv_h.at[:, at : at + n256], osem.at[k]
+            ),
+            SPREAD[2 * NC + 1 + h],
         )
 
     for load in loads[:2]:
@@ -413,23 +431,22 @@
 
         def ffn(i, _, c=c, cs=cs):
             slots(i, T // TT)
-
             r = rows_of(i * TT, TT)
+            if c:
+                keep_act(c - 1, i, r).wait()
             h = nn(N2[r, :], wu[:, cs])
             da = nt(DY[r, :], wd[cs, :])
             phi = 0.5 + 0.5 * lax.erf(h * 0.7071067811865476)
             slope = phi + h * (jnp.exp(h * h * -0.5) * 0.3989422804014327)
             d = (da * slope).astype(bf)
-            if c:
-                keep_act(c - 1, i, r).wait()
             ACT[r, :] = (h * phi).astype(bf)
-            keep_act(c, i, r).start()
             DH[r, :] = d
             d2 = nt(d, wu[:, cs])
             if c:
                 D2[r, :] += d2
             else:
                 D2[r, :] = d2
+            keep_act(c, i, r).start()
             return 0
 
         lax.fori_loop(0, T // TT, ffn, 0)
@@ -444,6 +461,7 @@
         slots(i, T // TT)
 
         r = rows_of(i * TT, TT)
+        keep_act(NC - 1, i, r).wait()
         d2 = D2[r, :]
         xhat, rstd = standardise(MID[r, :])
         SMALL[2:3, :] += jnp.sum(d2 * xhat, axis=0, keepdims=True)
@@ -451,7 +469,6 @@
         dmid = DY[r, :].astype(f32) + norm_grad(d2, xhat, rstd, gain2)
         D2[r, :] = dmid
         db = dmid.astype(bf)
-        keep_act(NC - 1, i, r).wait()
         ACT[r, :] = db
         DH[r, :] = nt(db, wo[...]).astype(bf)
         return 0
@@ -532,6 +549,8 @@
                 fetch.start()
         at = 768 * h
         N2T[:, at : at + 256] = nn(NT_[...], Q[:, c]).astype(bf)
+        reduce_part(h, 0)
+        slot()
         give_left.wait()
         give_right.wait()
         live_l = jnp.where(me < ntm - 1, 1.0, 0.0).astype(f32)
@@ -556,15 +575,12 @@
         N2T[:, at + 256 : at + 512] = (
             nn(NT_[...], KV[own, c]) + tn(SUMM[0:NS, :], N2[NS * h : NS * h + NS, 0:256])
         ).astype(bf)
+        reduce_part(h, 1)
+        slot()
         N2T[:, at + 512 : at + 768] = (
             nn(NT_[...], KV[own, cv]) + tn(SUMM[0:NS, :], N2[NS * h : NS * h + NS, 256:512])
         ).astype(bf)
-        reduce_block(
-            nu + h, ORDER[2 * NC + 1 + h],
-            lambda r, c, at=at: N2T.at[r, pl.ds(at + c.start, c.size)],
-            lambda r, c, h=h: UQR.at[h, r, c],
-            768,
-        )
+        reduce_part(h, 2)
         slot()
 
     dsum = jnp.zeros((NS, D), f32)
@@ -657,19 +673,15 @@
     lax.fori_loop(0, T // TT, down, 0)
     for k in range(T // TT, len(small_stages) + 1):
         small_step(k)
-    store_s = pltpu.make_async_copy(SMALL, small_h, osem.at[4])
+    store_s = pltpu.make_async_copy(SMALL, small_h, osem.at[2 * nu + 6])
     store_s.start()
     while active:
         slot(True)
-    store_u = pltpu.make_async_copy(U, units_h, osem.at[2])
-    store_q = pltpu.make_async_copy(N2T.at[:, 0 : 3 * D], uqkv_h, osem.at[3])
-    store_u.start()
-    store_q.start()
     for i in range(T // TT):
         r = pl.ds(i * TT, TT)
         give_back(i, r).wait()
         put_out(i, r).wait()
-    for store in (store_u, store_q, store_s):
+    for store in stored + [store_s]:
         store.wait()
 
 
@@ -716,9 +728,9 @@
         vm(2, 48, D, bf), vm(2, 16, D, bf), vm(2, 48, D, bf), vm(2, 16, D, bf),
         vm(nu, D, D, bf), vm(nu, land, D, bf), vm(2, land, 768, bf),
         vm(8, D, f32), vm(2 * levels, 8, D, f32),
-        dma(6), dma(5), dma(6), dma(6),
-        dma(2 * nu + 4, sems), dma(2 * nu + 4, sems), dma(2 * levels), dma(2 * levels),
-        pltpu.SemaphoreType.REGULAR((2 * nu + 4, levels)), dma(T // TT), dma(max(NC + 1, T // TT)),
+        dma(6), dma(2 * nu + 7), dma(6), dma(6),
+        dma(2 * nu + 6, sems), dma(2 * nu + 6, sems), dma(2 * levels), dma(2 * levels),
+        pltpu.SemaphoreType.REGULAR((2 * nu + 6, levels)), dma(T // TT), dma(max(NC + 1, T // TT)),
     ]
     row = lambda v: v.reshape(1, D)
     out, gframes, units, uqkv, small, _, _ = pl.pallas_call(
@@ -739,8 +751,7 @@
             vmem_limit_bytes=64 * 2**20 - 2**18, collective_id=0, has_side_effects=True
         ),
     )(frames[0], dy[0], wqkv, wo, wu, wd, lens, row(ga), row(ba), row(gf), row(bfn))
-    parts = FFC // 512
-    steps = NC * parts
+    steps = NC
     part, tile = D // steps, T // steps
     spec = lambda shape, index: pl.BlockSpec(shape, index)
     down, up, gout, gqkv, out, gframes, *vectors = pl.pallas_call(
@@ -756,8 +767,8 @@
         ]
         + [jax.ShapeDtypeStruct((1, D), f32)] * 4,
         in_specs=[
-            spec((1, D, 512), lambda k: (k // parts, 0, k % parts)),
-            spec((1, D, 512), lambda k: (NC + k // parts, 0, k % parts)),
+            spec((1, D, D), lambda k: (k, 0, 0)),
+            spec((1, D, D), lambda k: (NC + k, 0, 0)),
             spec((1, part, D), lambda k: (2 * NC, k, 0)),
             spec((part, 3 * D), lambda k: (k, 0)),
             spec((tile, D), lambda k: (k, 0)),
@@ -765,8 +776,8 @@
             spec((8, D), lambda k: (0, 0)),
         ],
         out_specs=[
-            spec((512, D), lambda k: (k, 0)),
-            spec((D, 512), lambda k: (0, k)),
+            spec((FFC, D), lambda k: (k, 0)),
+            spec((D, FFC), lambda k: (0, k)),
             spec((part, D), lambda k: (k, 0)),
             spec((part, 3 * D), lambda k: (k, 0)),
             spec((tile, D), lambda k: (k, 0)),

time: 146 us -> 142 us (0.973)
  Pallas kernels: 145 us -> 141 us
    pallas_call x1, Pallas kernels: 133 us -> 129 us  [local(): pl.pallas_call(functools.partial(body, ntm, (T, D, FF, NU)), out_shape=[j...]
where the time goes in v4:
time: 142 us
  Pallas kernels  141 us (99%)
    pallas_call x1, Pallas kernels, local(): pl.pallas_call(functools.partial(body, ntm, (T, D, FF, NU)), out_shape=[j...  129 us
    pallas_call x1, Pallas kernels, local(): pl.pallas_call(finish, grid=(steps,), out_shape=[jax.ShapeDtypeStruct((FF...  12 us

profile of v4, /device:TPU:0, one launch (start us, length us, event | category | flops | bytes accessed | tf_op | source)
XLA Modules:
  0.0 142.0 jit_solution(485898071076959944)
XLA Ops:
  0.6 129.1 %shard_map.186 = (bf16[2048,512]{1,0:T(8,128)(2,1)}, f32[2048,512]{1,0:T(8,128)}, bf16[9,512,512]{2,1,0:T(8,128)(2,1)}, bf16[512,1536]{1,0:T(8,128)(2,1)}, f32[8...) custom-call(bf16[2048,512]{1,0:T(8,128)(2,1)} %bitcast.12, bf16[2048,512]{1,0:T(8,128)(2,1)} %bitcast.13, ...), custom_call_target="tpu_custom_call" | custom-call | tf_op jit(solution)/shard_map/pallas_call | solution.py:736
  129.8 12.0 %shard_map.187 = (f32[2048,512]{1,0:T(8,128)}, f32[512,2048]{1,0:T(8,128)}, f32[512,512]{1,0:T(8,128)}, f32[512,1536]{1,0:T(8,128)}, bf16[2048,512]{1,0:T(8,128)...) custom-call(bf16[9,512,512]{2,1,0:T(8,128)(2,1)} %get-tuple-element., ...), custom_call_target="tpu_custom_call" | custom-call | tf_op jit(solution)/shard_map/pallas_call | solution.py:757

commit v5 on v4

--- a/solution.py
+++ b/solution.py
@@ -20,9 +20,9 @@
 bf = jnp.bfloat16
 f32 = jnp.float32
 MESH = pl.DeviceIdType.MESH
-ORDER = ["01"] * 9 + ["qqq", "qqq"]
+ORDER = ["01", "02", "01", "01", "01", "12", "01", "01", "01", "qqq", "qqq"]
 ENDS = [[2], [2]]
-SPREAD = [1.5, 1.4, 1.2, 1.0, 1.5, 1.4, 1.2, 1.0, 1.0, 1.0, 1.0]
+SPREAD = [1.3, 1.3, 1.2, 1.0, 1.3, 1.3, 1.2, 1.0, 1.0, 1.0, 1.0]
 GAPS = {
     "0": [1, 4, 3, 3, 4, 3, 3, 4, 1],
     "p": [1, 5, 3, 3, 3, 5, 1],

time: 142 us -> 141 us (level)
  no operation moved by 1% of the time
where the time goes in v5:
time: 141 us
  Pallas kernels  140 us (99%)
    pallas_call x1, Pallas kernels, local(): pl.pallas_call(functools.partial(body, ntm, (T, D, FF, NU)), out_shape=[j...  128 us
    pallas_call x1, Pallas kernels, local(): pl.pallas_call(finish, grid=(steps,), out_shape=[jax.ShapeDtypeStruct((FF...  12 us

profile of v5, /device:TPU:0, one launch (start us, length us, event | category | flops | bytes accessed | tf_op | source)
XLA Modules:
  0.0 141.0 jit_solution(12158774209870646676)
XLA Ops:
  0.6 128.1 %shard_map.186 = (bf16[2048,512]{1,0:T(8,128)(2,1)}, f32[2048,512]{1,0:T(8,128)}, bf16[9,512,512]{2,1,0:T(8,128)(2,1)}, bf16[512,1536]{1,0:T(8,128)(2,1)}, f32[8...) custom-call(bf16[2048,512]{1,0:T(8,128)(2,1)} %bitcast.12, bf16[2048,512]{1,0:T(8,128)(2,1)} %bitcast.13, ...), custom_call_target="tpu_custom_call" | custom-call | tf_op jit(solution)/shard_map/pallas_call | solution.py:736
  128.8 12.0 %shard_map.187 = (f32[2048,512]{1,0:T(8,128)}, f32[512,2048]{1,0:T(8,128)}, f32[512,512]{1,0:T(8,128)}, f32[512,1536]{1,0:T(8,128)}, bf16[2048,512]{1,0:T(8,128)...) custom-call(bf16[9,512,512]{2,1,0:T(8,128)(2,1)} %get-tuple-element., ...), custom_call_target="tpu_custom_call" | custom-call | tf_op jit(solution)/shard_map/pallas_call | solution.py:757

commit v6 on v5

--- a/solution.py
+++ b/solution.py
@@ -603,12 +603,12 @@
         xhat, rstd = standardise(X[r, :].astype(f32))
         SMALL[0:1, :] += jnp.sum(dn * xhat, axis=0, keepdims=True)
         SMALL[1:2, :] += jnp.sum(dn, axis=0, keepdims=True)
-        D2[r, :] += norm_grad(dn, xhat, rstd, gain1)
+        Q[r, :] = (D2[r, :] + norm_grad(dn, xhat, rstd, gain1)).astype(bf)
         give_back(i, r).start()
         return 0
 
     def give_back(i, r):
-        return pltpu.make_async_copy(D2.at[r], gframes_h.at[r], asem.at[i])
+        return pltpu.make_async_copy(Q.at[r], gframes_h.at[r], asem.at[i])
 
     lax.fori_loop(0, T // TT, back_in, 0)
 
@@ -697,7 +697,7 @@
                 :, 768 * h + 256 * p : 768 * h + 256 * p + 256
             ].astype(f32)
     out_o[...] = out[...]
-    gframes_o[...] = gframes[...]
+    gframes_o[...] = gframes[...].astype(f32)
 
 
 def local(frames, lens, wqkv, wo, wu, wd, ga, ba, gf, bfn, dy):
@@ -737,7 +737,7 @@
         functools.partial(body, ntm, (T, D, FF, NU)),
         out_shape=[
             jax.ShapeDtypeStruct((T, D), bf),
-            jax.ShapeDtypeStruct((T, D), f32),
+            jax.ShapeDtypeStruct((T, D), bf),
             jax.ShapeDtypeStruct((nu, D, D), bf),
             jax.ShapeDtypeStruct((D, 3 * D), bf),
             jax.ShapeDtypeStruct((8, D), f32),

time: 141 us -> 140 us (level)
  no operation moved by 1% of the time
where the time goes in v6:
time: 140 us
  Pallas kernels  139 us (99%)
    pallas_call x1, Pallas kernels, local(): pl.pallas_call(functools.partial(body, ntm, (T, D, FF, NU)), out_shape=[j...  128 us
    pallas_call x1, Pallas kernels, local(): pl.pallas_call(finish, grid=(steps,), out_shape=[jax.ShapeDtypeStruct((FF...  11.3 us

profile of v6, /device:TPU:0, one launch (start us, length us, event | category | flops | bytes accessed | tf_op | source)
XLA Modules:
  0.0 140.2 jit_solution(3131721697195157987)
XLA Ops:
  0.6 128.1 %shard_map.186 = (bf16[2048,512]{1,0:T(8,128)(2,1)}, bf16[2048,512]{1,0:T(8,128)(2,1)}, bf16[9,512,512]{2,1,0:T(8,128)(2,1)}, bf16[512,1536]{1,0:T(8,128)(2,1)},...) custom-call(bf16[2048,512]{1,0:T(8,128)(2,1)} %bitcast.12, bf16[2048,512]{1,0:T(8,128)(2,1)} %bitcast.13, ...), custom_call_target="tpu_custom_call" | custom-call | tf_op jit(solution)/shard_map/pallas_call | solution.py:736
  128.8 11.3 %shard_map.187 = (f32[2048,512]{1,0:T(8,128)}, f32[512,2048]{1,0:T(8,128)}, f32[512,512]{1,0:T(8,128)}, f32[512,1536]{1,0:T(8,128)}, bf16[2048,512]{1,0:T(8,128)...) custom-call(bf16[9,512,512]{2,1,0:T(8,128)(2,1)} %get-tuple-element., ...), custom_call_target="tpu_custom_call" | custom-call | tf_op jit(solution)/shard_map/pallas_call | solution.py:757
